TPU v7x, 256 devices: a whole 4x4x8 slice. The times are simulated.
256 devices in a mesh: dp: 64 (over z_hi, x, y, core), mp: 4 (over z_lo).
Axes of the slice: x: 4, y: 4, z: 8 (z_hi: 2, z_lo: 4; z = z_hi * 4 + z_lo), core: 2. Of those that a mesh axis runs over, the one named last changes fastest.
Arguments:
- tokens: bfloat16 [8192, 3072], P('dp', 'mp'), may hold values from -16 to 16
- weight: bfloat16 [3072, 12288], P('dp', 'mp'), may hold values from -0.109375 to 0.109375
- logits: float32 [6, 768, 12288], P(None, 'dp', 'mp'), may hold values from -8 to 320
- gumbel: bfloat16 [6, 768, 12288], P(None, 'dp', 'mp'), may hold values from -2 to 7, as said below
- cotangent: bfloat16 [8192, 12288], P('dp', 'mp'), may hold values from -6 to 6
- moment_one: float32 [6, 768, 12288], P(None, 'dp', 'mp'), may hold values from -6 to 6
- moment_two: float32 [6, 768, 12288], P(None, 'dp', 'mp'), may hold values from 0.01 to 1
Outputs:
- output: bfloat16 [8192, 12288], P('dp', 'mp')
- input_grad: bfloat16 [8192, 3072], P('dp', 'mp')
- new_logits: float32 [6, 768, 12288], P(None, 'dp', 'mp')
- new_moment_one: float32 [6, 768, 12288], P(None, 'dp', 'mp')
- new_moment_two: float32 [6, 768, 12288], P(None, 'dp', 'mp')
Inputs may be any that keep to these rules, and one draw needn't show every extreme that they name: `gumbel`: Gumbel(0, 1) noise.
All inputs are finite; a program needn't handle non-finite values.
Results may differ from a plain program's by a relative error of at most 0.002.
The roundings to bfloat16 on the way count: a program that leaves them out, or rounds other values in their place, can miss the bound.
Values may be sent and summed in bfloat16 or wider, within the bound.
No kernel may reach another device: no remote copies, remote signals or barrier semaphores. Data moves between devices by JAX's collectives and lax.ppermute only.
A program may use at most 128 MiB of HBM per device.

v0:
```python
import functools
import math

import jax
import jax.numpy as jnp
import numpy as np
from jax import lax
from jax.experimental import pallas as pl
from jax.experimental.pallas import tpu as pltpu
from jax.sharding import PartitionSpec as P

beta_one = 0.9
beta_two = 0.999
adam_eps = 1e-08
decay = 0.01
rate = 0.1
adam_step = 10.0

F32 = jnp.float32
BF16 = jnp.bfloat16
AXES = ("dp", "mp")
SIZES = (2, 4, 4, 2, 4)
PAIRS = tuple((i, j) for i in range(4) for j in range(i + 1, 4))
ROWS = 48
HALF = 1536
WIDE = 512
TILE = 512
MIB = 1 << 20
IN_VMEM = pl.BlockSpec(memory_space=pltpu.VMEM)


def pairs_of(target):
    found = []
    for here in np.ndindex(*SIZES):
        there = tuple(a % b for a, b in zip(target(*here), SIZES))
        found.append(
            (int(np.ravel_multi_index(here, SIZES)), int(np.ravel_multi_index(there, SIZES)))
        )
    return found


def step_a(by):
    return pairs_of(
        lambda z, x, y, c, m: (z, x + by, y, c, m) if c == 0 else (z, x, y + by, c, m)
    )


def step_b(by):
    return pairs_of(
        lambda z, x, y, c, m: (z, x, y + by, c, m) if c == 0 else (z, x + by, y, c, m)
    )


SIBLING = pairs_of(lambda z, x, y, c, m: (z, x, y, c + 1, m))
PARTNER = pairs_of(lambda z, x, y, c, m: (z + 1, x, y, c, m))
A_UP, A_DOWN, A_TWO = step_a(1), step_a(-1), step_a(2)
B_UP, B_DOWN = step_b(1), step_b(-1)


def around(by):
    return pairs_of(lambda z, x, y, c, m: (z, x, y, c, m + by))


def send(value, pairs):
    return lax.ppermute(value, AXES, pairs)


def dot(a, b, dims):
    return lax.dot_general(a, b, (dims, ((), ())), preferred_element_type=F32)


def mask_kernel(logits, gumbel, weight, probs, masked, spread):
    scores = [logits[p] + gumbel[p].astype(F32) for p in range(6)]
    top = scores[0]
    for p in range(1, 6):
        top = jnp.maximum(top, scores[p])
    exps = [jnp.exp(s - top) for s in scores]
    total = exps[0]
    for p in range(1, 6):
        total = total + exps[p]
    share = [e / total for e in exps]
    for p in range(6):
        probs[p] = share[p]
    for slot in range(4):
        kept = [share[p] for p in range(6) if slot in PAIRS[p]]
        mask = kept[0] + kept[1] + kept[2]
        for j in range(WIDE // 128):
            at = j * 128
            spread[pl.ds(j * ROWS + slot, 12, stride=4), :] = mask[:, at : at + 128]
    for j in range(WIDE // 128):
        at = j * 128
        part = weight[:, at : at + 128].astype(F32) * spread[j * ROWS : (j + 1) * ROWS, :]
        masked[:, at : at + 128] = part.astype(BF16)


def make_masked(logits, gumbel, weight):
    cols = weight.shape[1]
    wide = WIDE
    three = pl.BlockSpec((6, 12, wide), lambda i: (0, 0, i))
    two = pl.BlockSpec((ROWS, wide), lambda i: (0, i))
    return pl.pallas_call(
        mask_kernel,
        grid=(cols // wide,),
        in_specs=[three, three, two],
        out_specs=[three, two],
        out_shape=[
            jax.ShapeDtypeStruct((6, 12, cols), F32),
            jax.ShapeDtypeStruct((ROWS, cols), BF16),
        ],
        scratch_shapes=[pltpu.VMEM((wide // 128 * ROWS, 128), F32)],
        compiler_params=pltpu.CompilerParams(vmem_limit_bytes=16 * MIB),
        cost_estimate=pl.CostEstimate(flops=8000000, bytes_accessed=2800000, transcendentals=221184),
    )(logits, gumbel, weight)


def adam_kernel(wgrad, weight, probs, logits, one, two, new_logits, new_one, new_two, spread):
    for j in range(WIDE // 128):
        at = j * 128
        spread[j * ROWS : (j + 1) * ROWS, :] = (
            weight[:, at : at + 128].astype(F32) * wgrad[:, at : at + 128]
        )
    slots = [
        jnp.concatenate(
            [spread[pl.ds(j * ROWS + slot, 12, stride=4), :] for j in range(WIDE // 128)], axis=1
        )
        for slot in range(4)
    ]
    pgrad = [slots[i] + slots[j] for i, j in PAIRS]
    share = [probs[p] for p in range(6)]
    mean = share[0] * pgrad[0]
    for p in range(1, 6):
        mean = mean + share[p] * pgrad[p]
    for p in range(6):
        lgrad = share[p] * (pgrad[p] - mean)
        first = beta_one * one[p] + (1.0 - beta_one) * lgrad
        second = beta_two * two[p] + (1.0 - beta_two) * lgrad * lgrad
        new_one[p] = first
        new_two[p] = second
        first_hat = first / (1.0 - beta_one**adam_step)
        second_hat = second / (1.0 - beta_two**adam_step)
        old = logits[p]
        new_logits[p] = old - rate * (first_hat / (jnp.sqrt(second_hat) + adam_eps) + decay * old)


def adam(wgrad, weight, probs, logits, one, two):
    cols = weight.shape[1]
    wide = WIDE
    three = pl.BlockSpec((6, 12, wide), lambda i: (0, 0, i))
    flat = pl.BlockSpec((ROWS, wide), lambda i: (0, i))
    out = jax.ShapeDtypeStruct((6, 12, cols), F32)
    return pl.pallas_call(
        adam_kernel,
        grid=(cols // wide,),
        in_specs=[flat, flat, three, three, three, three],
        out_specs=[three, three, three],
        out_shape=[out, out, out],
        scratch_shapes=[pltpu.VMEM((wide // 128 * ROWS, 128), F32)],
        compiler_params=pltpu.CompilerParams(vmem_limit_bytes=16 * MIB),
        cost_estimate=pl.CostEstimate(flops=8000000, bytes_accessed=7000000, transcendentals=221184),
    )(wgrad, weight, probs, logits, one, two)


def meet_kernel(place, mine, other, out):
    for i in range(64):
        at = pl.multiple_of(place[i] * ROWS, ROWS)
        out[pl.ds(at, ROWS), :128] = mine[i * ROWS : (i + 1) * ROWS, :]
        out[pl.ds(at, ROWS), 128:] = other[i * ROWS : (i + 1) * ROWS, :]


def meet(place, mine, other):
    return pl.pallas_call(
        meet_kernel,
        in_specs=[pl.BlockSpec(memory_space=pltpu.SMEM)] + [IN_VMEM] * 2,
        out_specs=IN_VMEM,
        out_shape=jax.ShapeDtypeStruct((3072, 256), BF16),
        compiler_params=pltpu.CompilerParams(vmem_limit_bytes=16 * MIB),
        cost_estimate=pl.CostEstimate(flops=0, bytes_accessed=3200000, transcendentals=0),
    )(place, mine, other)


def part_kernel(place, *refs):
    mine, other = refs[-2:]
    at_block = 0
    for ref in refs[:-2]:
        for i in range(ref.shape[0] // ROWS):
            at = pl.multiple_of(place[at_block] * ROWS, ROWS)
            mine[pl.ds(at, ROWS), :] = ref[i * ROWS : (i + 1) * ROWS, :128]
            other[pl.ds(at, ROWS), :] = ref[i * ROWS : (i + 1) * ROWS, 128:]
            at_block += 1


def part(place, pieces):
    out = jax.ShapeDtypeStruct((3072, 128), F32)
    return pl.pallas_call(
        part_kernel,
        in_specs=[pl.BlockSpec(memory_space=pltpu.SMEM)] + [IN_VMEM] * len(pieces),
        out_specs=[IN_VMEM] * 2,
        out_shape=[out, out],
        compiler_params=pltpu.CompilerParams(vmem_limit_bytes=16 * MIB),
        cost_estimate=pl.CostEstimate(flops=0, bytes_accessed=6400000, transcendentals=0),
    )(place, *pieces)


def share(acts, cot, start, count, at):
    return dot(acts[start : start + count, :], cot[:, at : at + TILE], ((1,), (0,)))


def line_kernel(*refs):
    out = refs[-1]
    for i, ref in enumerate(refs[:-1]):
        out[i * 96 : (i + 1) * 96, :] = ref[...]


def lead_kernel(start, acts, cot, near, far, up, down):
    up[:192, :] = far[192:384, :]
    down[:192, :] = near[:192, :]
    for at in range(0, HALF, TILE):
        cols = slice(at, at + TILE)
        up[192:, cols] = share(acts, cot, start, 192, at).astype(BF16)
        down[192:, cols] = share(acts, cot, start + 192, 192, at).astype(BF16)


def follow_kernel(start_up, start_down, acts, cot, low, high, *refs):
    up, down = refs[-2:]
    base = 96 * (len(refs) - 2)
    for i, ref in enumerate(refs[:-2]):
        up[i * 96 : (i + 1) * 96, :] = ref[...]
        down[i * 96 : (i + 1) * 96, :] = ref[...]
    for at in range(0, HALF, TILE):
        cols = slice(at, at + TILE)
        got = share(acts, cot, start_up, 192, at) + low[192:, cols].astype(F32)
        up[base : base + 192, cols] = got.astype(BF16)
        up[base + 192 :, cols] = share(acts, cot, start_up + 192, 192, at).astype(BF16)
        down[base : base + 192, cols] = share(acts, cot, start_down, 192, at).astype(BF16)
        got = share(acts, cot, start_down + 192, 192, at) + high[192:, cols].astype(F32)
        down[base + 192 :, cols] = got.astype(BF16)


def keep_kernel(start, acts, cot, up, down, own, *others):
    base = up.shape[0] - 384
    for at in range(0, HALF, TILE):
        cols = slice(at, at + TILE)
        for i in range(4):
            rows = slice(base + i * 96, base + i * 96 + 96)
            got = share(acts, cot, start + i * 96, 96, at)
            got = got + up[rows, cols].astype(F32) + down[rows, cols].astype(F32)
            if i == 0:
                own[:, cols] = got
            else:
                others[i - 1][:, cols] = got.astype(BF16)


def in_vmem(kernel, out_shape, flops, *args):
    moved = sum(a.size * a.dtype.itemsize for a in args)
    moved += sum(math.prod(o.shape) * o.dtype.itemsize for o in out_shape)
    return pl.pallas_call(
        kernel,
        in_specs=[IN_VMEM] * len(args),
        out_specs=[IN_VMEM] * len(out_shape),
        out_shape=out_shape,
        compiler_params=pltpu.CompilerParams(vmem_limit_bytes=24 * MIB),
        cost_estimate=pl.CostEstimate(flops=flops, bytes_accessed=moved, transcendentals=0),
    )(*args)


def shape16(rows):
    return jax.ShapeDtypeStruct((rows, HALF), BF16)


def product_kernel(starts, counts, first, acts, cot, *refs):
    size = len(starts)
    before = None if first else refs[0]
    refs = refs if first else refs[1:]
    pieces, result, grads = refs[:size], refs[size], refs[size + 1 :]
    for at in range(0, HALF, TILE):
        cols = slice(at, at + TILE)
        total = None if first else before[:, cols]
        for start, count, piece in zip(starts, counts, pieces):
            term = dot(acts[start : start + count, :], piece[:count, cols], ((0,), (0,)))
            total = term if total is None else total + term
        result[:, cols] = total
    for count, piece, grad in zip(counts, pieces, grads):
        grad[...] = dot(piece[:count, :], cot[...], ((1,), (1,)))


def products(acts, cot, before, starts, counts, pieces):
    first = before is None
    shapes = [jax.ShapeDtypeStruct((256, HALF), F32)]
    shapes += [jax.ShapeDtypeStruct((n, 256), F32) for n in counts]
    args = [acts, cot] + ([] if first else [before]) + pieces
    return in_vmem(
        functools.partial(product_kernel, starts, counts, first),
        shapes, 4 * sum(counts) * 256 * HALF, *args
    )


def local(tokens, weight, logits, gumbel, cotangent, moment_one, moment_two):
    dp = lax.axis_index("dp")
    mp = lax.axis_index("mp")
    core, y, x, zh = dp % 2, (dp // 2) % 4, (dp // 8) % 4, dp // 32

    def half(value, which):
        return lax.dynamic_slice_in_dim(value, which * HALF, HALF, axis=1)

    whole = np.arange(64)
    dx, dy = (whole // 8 - x) % 4, (whole // 2 - y) % 4
    da, db = jnp.where(core == 0, dx, dy), jnp.where(core == 0, dy, dx)
    met_at = ((((whole // 32) ^ zh) * 4 + db) * 4 + da) * 2 + ((whole % 2) ^ core)
    met_at = met_at.astype(jnp.int32)
    order = np.arange(64)
    oz, ob, oa, oc = order // 32, (order // 8) % 4, (order // 2) % 4, order % 2
    ox, oy = jnp.where(core == 0, oa, ob), jnp.where(core == 0, ob, oa)
    lies_at = (((oz ^ zh) * 4 + (ox + x) % 4) * 4 + (oy + y) % 4) * 2 + (oc ^ core)
    lies_at = lies_at.astype(jnp.int32)

    probs, masked = make_masked(logits, gumbel, weight)
    block = jnp.concatenate([half(masked, core), send(half(masked, 1 - core), SIBLING)], axis=0)
    blocks = [block, send(block, PARTNER)]

    flipped = tokens.T
    own = jnp.concatenate([flipped] + [send(flipped, around(r)) for r in (1, 2, 3)], axis=0)
    others = send(own, SIBLING)
    came = jnp.concatenate([((mp - r) % 4) * 16 + np.arange(16) for r in range(4)])
    acts = meet(met_at[came], own, others)
    cot = jnp.concatenate(
        [half(cotangent, core), send(half(cotangent, 1 - core), SIBLING)], axis=0
    )

    def start_of(dz, db):
        return (dz * 4 + db) * 384

    def spread_a(mine):
        return [mine, send(mine, A_DOWN), send(mine, A_TWO), send(mine, A_UP)]

    def kept(dz, up, down):
        own, one, two, three = in_vmem(
            functools.partial(keep_kernel, start_of(dz, 0)),
            [jax.ShapeDtypeStruct((96, HALF), F32)] + [shape16(96)] * 3, work, acts, cot, up, down,
        )
        one, two, three = send(one, A_UP), send(two, A_TWO), send(three, A_DOWN)
        return own + one.astype(F32) + two.astype(F32) + three.astype(F32)

    work = 2 * 384 * 256 * HALF
    line0 = in_vmem(line_kernel, [shape16(384)], 0, *spread_a(blocks[0]))[0]
    near0, far0 = send(line0, B_DOWN), send(line0, B_UP)
    up, down = in_vmem(
        functools.partial(lead_kernel, start_of(1, 2)), [shape16(384)] * 2, work, acts, cot, near0, far0
    )
    high0, low0 = send(up, B_UP), send(down, B_DOWN)
    line1, down = in_vmem(
        functools.partial(follow_kernel, start_of(1, 1), start_of(1, 3)),
        [shape16(768)] * 2, 2 * work, acts, cot, high0, low0, *spread_a(blocks[1]),
    )
    far1, near1 = send(line1, B_UP), send(down, B_DOWN)
    up, down = in_vmem(
        functools.partial(lead_kernel, start_of(0, 2)), [shape16(384)] * 2, work, acts, cot, near1, far1
    )
    high1, low1 = send(up, B_UP), send(down, B_DOWN)
    sums = {1: kept(1, far1, near1)}
    up, down = in_vmem(
        functools.partial(follow_kernel, start_of(0, 1), start_of(0, 3)),
        [shape16(384)] * 2, 2 * work, acts, cot, high1, low1,
    )
    up, down = send(up, B_UP), send(down, B_DOWN)
    sums[0] = kept(0, up, down)
    wsum = sums[0] + send(sums[1].astype(BF16), PARTNER).astype(F32)
    other = send(wsum[ROWS:], SIBLING)
    wgrad = jnp.where(
        core == 0,
        jnp.concatenate([wsum[:ROWS], other], axis=1),
        jnp.concatenate([other, wsum[:ROWS]], axis=1),
    )
    new_logits, new_one, new_two = adam(wgrad, weight, probs, logits, moment_one, moment_two)

    near = [start_of(dz, db) for dz in range(2) for db in (0, 1, 3)]
    opposite = [(start_of(dz, 2), start_of(dz, 2) + 192) for dz in range(2)]
    result, g0, g1, g3, g2, g4 = products(
        acts, cot, None, near[:3] + list(opposite[0]), [384] * 3 + [192] * 2,
        [line0, near0, far0, low0, high0],
    )
    result, h0, h1, h3 = products(
        acts, cot, result, near[3:], [384] * 3, [line1, near1, far1]
    )
    result, h2, h4 = products(acts, cot, result, opposite[1], [192] * 2, [low1, high1])
    grads = [g0, g1, g2, g4, g3, h0, h1, h2, h4, h3]
    result = result.astype(BF16)
    other = send(result[128:], SIBLING)
    output = jnp.where(
        core == 0,
        jnp.concatenate([result[:128], other], axis=1),
        jnp.concatenate([other, result[:128]], axis=1),
    )

    mine, theirs = part(lies_at, grads)
    grad = mine + send(theirs, SIBLING)

    def quarter(r):
        return lax.dynamic_slice_in_dim(grad, ((mp + r) % 4) * 768, 768, axis=0)

    total = quarter(0)
    for r in (1, 2, 3):
        total = total + send(quarter(r), around(r))
    input_grad = total.astype(BF16).T
    return (output, input_grad, new_logits, new_one, new_two)


def solution(mesh):
    placed = (
        P("dp", "mp"),
        P("dp", "mp"),
        P(None, "dp", "mp"),
        P(None, "dp", "mp"),
        P("dp", "mp"),
        P(None, "dp", "mp"),
        P(None, "dp", "mp"),
    )
    return jax.shard_map(
        local,
        mesh=mesh,
        in_specs=placed,
        out_specs=(
            P("dp", "mp"),
            P("dp", "mp"),
            P(None, "dp", "mp"),
            P(None, "dp", "mp"),
            P(None, "dp", "mp"),
        ),
        check_vma=False,
    )
```

profile of v0, /device:TPU:1, one launch (start us, length us, event | category | flops | bytes accessed | tf_op | source)
XLA Modules:
  0.0 211.8 jit_solution(9191643549243062413)
XLA Ops:
  0.7 1.3 copy-done.6
  2.9 1.1 copy-done.24
  4.9 3.3 %collective-permute-start.5 = (bf16[48,1536]{1,0:T(8,128)(2,1)S(1)}, bf16[48,1536]{1,0:T(8,128)(2,1)S(1)}, u32[]{:S(2)}, u32[]{:S(2)}) collective-permute-start(bf16[48,1536]{1,0:T(8,128)(2,1)S(1)} %get-tuple-element.97), channel_id=1, source_target_pairs={{0,4},{1,5},{2,6},{3,7},{4,0},{5,1},{6,2},{7,3},{8,12},{9,13},{10,... | collective-permute-start | bytes 442376 | tf_op jit(solution)/shard_map/ppermute | solution.py:65
  8.3 1.0 collective-permute-done.5
  9.4 2.2 %collective-permute-start.7 = (bf16[96,1536]{1,0:T(8,128)(2,1)S(1)}, bf16[96,1536]{1,0:T(8,128)(2,1)S(1)}, u32[]{:S(2)}, u32[]{:S(2)}) collective-permute-start(bf16[96,1536]{1,0:T(8,128)(2,1)S(1)} %pad_maximum_fusion.2.refs_0_), channel_id=1, source_target_pairs={{0,64},{1,65},{2,66},{3,67},{4,20},{5,21},{6,22},{7,23},{8,72},{9,... | collective-permute-start | bytes 884744 | tf_op jit(solution)/shard_map/ppermute | solution.py:65
  11.6 1.1 collective-permute-start.6
  12.8 4.4 %collective-permute-start.2 = (bf16[768,128]{1,0:T(8,128)(2,1)S(1)}, bf16[768,128]{1,0:T(8,128)(2,1)}, u32[]{:S(2)}, u32[]{:S(2)}) collective-permute-start(bf16[768,128]{1,0:T(8,128)(2,1)S(1)} %bitcast.13), channel_id=1, source_target_pairs={{0,3},{1,0},{2,1},{3,2},{4,7},{5,4},{6,5},{7,6},{8,11},{9,8},{10,9... | collective-permute-start | bytes 589832 | tf_op jit(solution)/shard_map/ppermute | solution.py:65
  17.2 2.4 %collective-permute-done.8.refs_3_ = bf16[96,1536]{1,0:T(8,128)(2,1)S(1)} collective-permute-done((bf16[96,1536]{1,0:T(8,128)(2,1)S(1)}, bf16[96,1536]{1,0:T(8,128)(2,1)S(1)}, u32[]{:S(2)}, u32[]{:S(2)}) %collective-permute-start.8) | collective-permute-done | bytes 294944 | tf_op jit(solution)/shard_map/ppermute | solution.py:65
  20.5 1.1 shard_map.220.refs_0_
  21.6 2.7 %collective-permute-start.9 = (bf16[384,1536]{1,0:T(8,128)(2,1)}, bf16[384,1536]{1,0:T(8,128)(2,1)}, u32[]{:S(2)}, u32[]{:S(2)}) collective-permute-start(bf16[384,1536]{1,0:T(8,128)(2,1)} %shard_map.220.refs_0_), channel_id=1, source_target_pairs={{0,24},{1,25},{2,26},{3,27},{4,100},{5,101},{6,102},{7,103},{8,0},... | collective-permute-start | bytes 3538952 | tf_op jit(solution)/shard_map/ppermute | solution.py:65
  24.3 1.8 collective-permute-start.4
  26.1 7.3 %collective-permute-done.1 = bf16[768,128]{1,0:T(8,128)(2,1)} collective-permute-done((bf16[768,128]{1,0:T(8,128)(2,1)S(1)}, bf16[768,128]{1,0:T(8,128)(2,1)}, u32[]{:S(2)}, u32[]{:S(2)}) %collective-permute-start.1) | collective-permute-done | bytes 196640 | tf_op jit(solution)/shard_map/ppermute | solution.py:65
  33.4 1.2 pad_maximum_fusion.mine
  34.5 1.2 collective-permute-start.3
  36.7 1.1 pad_maximum_fusion.1.cot
  38.6 1.1 copy-done.23
  40.6 2.2 %shard_map.221 = (bf16[384,1536]{1,0:T(8,128)(2,1)S(1)}, bf16[384,1536]{1,0:T(8,128)(2,1)S(1)}) custom-call(bf16[3072,256]{1,0:T(8,128)(2,1)S(1)} %shard_map.218.acts, bf16[256,1536]{1,0:T(8,128)(2,1)S(1)} %pad_maximum_fusion.1.cot, bf16[384,1536]{1,0:T(8,128)(2,1)} %collective-permute-done.9.near.refs_1_, bf16[384,1536]{1,0:T(8,128)(2,1)} %collective-permute-done.10.far.refs_2_), custom_call_target="tpu_custom_call" | custom-call | flops 301989888 | bytes 7077888 | tf_op jit(solution)/shard_map/pallas_call | solution.py:256
  44.4 5.8 %collective-permute-start.13 = (bf16[96,1536]{1,0:T(8,128)(2,1)S(1)}, bf16[96,1536]{1,0:T(8,128)(2,1)S(1)}, u32[]{:S(2)}, u32[]{:S(2)}) collective-permute-start(bf16[96,1536]{1,0:T(8,128)(2,1)S(1)} %pad_maximum_fusion.2.refs_0_), channel_id=1, source_target_pairs={{0,128},{1,129},{2,130},{3,131},{4,132},{5,133},{6,134},{7,135},{8... | collective-permute-start | bytes 884744 | tf_op jit(solution)/shard_map/ppermute | solution.py:65
  50.2 5.8 %collective-permute-done.13.refs_0_ = bf16[96,1536]{1,0:T(8,128)(2,1)S(1)} collective-permute-done((bf16[96,1536]{1,0:T(8,128)(2,1)S(1)}, bf16[96,1536]{1,0:T(8,128)(2,1)S(1)}, u32[]{:S(2)}, u32[]{:S(2)}) %collective-permute-start.13) | collective-permute-done | bytes 294944 | tf_op jit(solution)/shard_map/ppermute | solution.py:65
  56.0 1.6 collective-permute-start.16
  57.5 2.4 %collective-permute-start.14 = (bf16[96,1536]{1,0:T(8,128)(2,1)S(1)}, bf16[96,1536]{1,0:T(8,128)(2,1)S(1)}, u32[]{:S(2)}, u32[]{:S(2)}) collective-permute-start(bf16[96,1536]{1,0:T(8,128)(2,1)S(1)} %collective-permute-done.13.refs_0_), channel_id=1, source_target_pairs={{0,96},{1,97},{2,98},{3,99},{4,28},{5,29},{6,30},{7,31},{8,104},{9... | collective-permute-start | bytes 884744 | tf_op jit(solution)/shard_map/ppermute | solution.py:65
  59.9 9.4 %collective-permute-done.16.refs_3_ = bf16[96,1536]{1,0:T(8,128)(2,1)S(1)} collective-permute-done((bf16[96,1536]{1,0:T(8,128)(2,1)S(1)}, bf16[96,1536]{1,0:T(8,128)(2,1)S(1)}, u32[]{:S(2)}, u32[]{:S(2)}) %collective-permute-start.16) | collective-permute-done | bytes 294944 | tf_op jit(solution)/shard_map/ppermute | solution.py:65
  70.8 2.3 %collective-permute-start.17 = (bf16[768,1536]{1,0:T(8,128)(2,1)S(1)}, bf16[768,1536]{1,0:T(8,128)(2,1)S(1)}, u32[]{:S(2)}, u32[]{:S(2)}) collective-permute-start(bf16[768,1536]{1,0:T(8,128)(2,1)S(1)} %get-tuple-element.46), channel_id=1, source_target_pairs={{0,24},{1,25},{2,26},{3,27},{4,100},{5,101},{6,102},{7,103},{8,0},... | collective-permute-start | bytes 7077896 | tf_op jit(solution)/shard_map/ppermute | solution.py:65
  73.1 1.4 copy-done.10
  74.5 26.2 %collective-permute-done.17.refs_2_.near.down = bf16[768,1536]{1,0:T(8,128)(2,1)S(1)} collective-permute-done((bf16[768,1536]{1,0:T(8,128)(2,1)S(1)}, bf16[768,1536]{1,0:T(8,128)(2,1)S(1)}, u32[]{:S(2)}, u32[]{:S(2)}) %collective-permute-start.17) | collective-permute-done | bytes 2359328 | tf_op jit(solution)/shard_map/ppermute | solution.py:65
  100.6 1.6 collective-permute-done.18.refs_3_.far.up
  103.7 1.4 collective-permute-start.19
  105.2 13.9 %collective-permute-done.19.refs_1_.high = bf16[384,1536]{1,0:T(8,128)(2,1)S(1)} collective-permute-done((bf16[384,1536]{1,0:T(8,128)(2,1)S(1)}, bf16[384,1536]{1,0:T(8,128)(2,1)S(1)}, u32[]{:S(2)}, u32[]{:S(2)}) %collective-permute-start.19) | collective-permute-done | bytes 1179680 | tf_op jit(solution)/shard_map/ppermute | solution.py:65
  119.1 2.6 %collective-permute-done.20.refs_2_.low = bf16[384,1536]{1,0:T(8,128)(2,1)S(1)} collective-permute-done((bf16[384,1536]{1,0:T(8,128)(2,1)S(1)}, bf16[384,1536]{1,0:T(8,128)(2,1)S(1)}, u32[]{:S(2)}, u32[]{:S(2)}) %collective-permute-start.20) | collective-permute-done | bytes 1179680 | tf_op jit(solution)/shard_map/ppermute | solution.py:65
  121.7 2.1 shard_map.228
  123.8 2.7 %collective-permute-start.27 = (bf16[384,1536]{1,0:T(8,128)(2,1)}, bf16[384,1536]{1,0:T(8,128)(2,1)}, u32[]{:S(2)}, u32[]{:S(2)}) collective-permute-start(bf16[384,1536]{1,0:T(8,128)(2,1)} %get-tuple-element.64), channel_id=1, source_target_pairs={{0,24},{1,25},{2,26},{3,27},{4,100},{5,101},{6,102},{7,103},{8,0},... | collective-permute-start | bytes 3538952 | tf_op jit(solution)/shard_map/ppermute | solution.py:65
  126.4 1.7 copy-done.1
  128.1 1.7 copy-done.4
  130.7 2.0 collective-permute-start.32
  133.2 5.3 %shard_map.222 = (f32[256,1536]{1,0:T(8,128)S(1)}, f32[384,256]{1,0:T(8,128)S(1)}, f32[384,256]{1,0:T(8,128)S(1)}, f32[384,256]{1,0:T(8,128)S(1)}, f32[192,256]{1,0:T(8,128)S(1)}, /*index=5*/f32[192,256]{1,0:T(8,128)S(1)}) custom-call(bf16[3072,256]{1,0:T(8,128)(2,1)S(1)} %shard_map.218.acts, bf16[256,1536]{1,0:T(8,128)(2,1)S(1)} %pad_maximum_fusion.1.cot, ...), custom_call_target="tpu_custom_call" | custom-call | flops 2415919104 | bytes 11403264 | tf_op jit(solution)/shard_map/pallas_call | solution.py:256
  138.6 2.3 %shard_map.224 = (f32[256,1536]{1,0:T(8,128)S(1)}, f32[384,256]{1,0:T(8,128)S(1)}, f32[384,256]{1,0:T(8,128)S(1)}, f32[384,256]{1,0:T(8,128)S(1)}) custom-call(bf16[3072,256]{1,0:T(8,128)(2,1)S(1)} %shard_map.218.acts, bf16[256,1536]{1,0:T(8,128)(2,1)S(1)} %pad_maximum_fusion.1.cot, f32[256,1536]{1,0:T(8,128)S(1)} %get-tuple-element.44.refs_0_, ...), custom_call_target="tpu_custom_call" | custom-call | flops 1811939328 | bytes 13762560 | tf_op jit(solution)/shard_map/pallas_call | solution.py:256
  140.9 1.1 shard_map.226
  142.7 12.3 %collective-permute-start.22 = (f32[3072,128]{1,0:T(8,128)S(1)}, f32[3072,128]{1,0:T(8,128)S(1)}, u32[]{:S(2)}, u32[]{:S(2)}) collective-permute-start(f32[3072,128]{1,0:T(8,128)S(1)} %get-tuple-element.62), channel_id=1, source_target_pairs={{0,4},{1,5},{2,6},{3,7},{4,0},{5,1},{6,2},{7,3},{8,12},{9,13},{10,... | collective-permute-start | bytes 4718600 | tf_op jit(solution)/shard_map/ppermute | solution.py:65
  155.2 6.4 %collective-permute-start.34 = (bf16[96,1536]{1,0:T(8,128)(2,1)S(1)}, bf16[96,1536]{1,0:T(8,128)(2,1)S(1)}, u32[]{:S(2)}, u32[]{:S(2)}) collective-permute-start(bf16[96,1536]{1,0:T(8,128)(2,1)S(1)} %add_convert_fusion), channel_id=1, source_target_pairs={{0,128},{1,129},{2,130},{3,131},{4,132},{5,133},{6,134},{7,135},{8... | collective-permute-start | bytes 884744 | tf_op jit(solution)/shard_map/ppermute | solution.py:65
  161.8 2.3 %shard_map.229 = (f32[96,1536]{1,0:T(8,128)S(1)}, bf16[96,1536]{1,0:T(8,128)(2,1)S(1)}, bf16[96,1536]{1,0:T(8,128)(2,1)S(1)}, bf16[96,1536]{1,0:T(8,128)(2,1)S(1)}) custom-call(bf16[3072,256]{1,0:T(8,128)(2,1)S(1)} %shard_map.218.acts, bf16[256,1536]{1,0:T(8,128)(2,1)S(1)} %pad_maximum_fusion.1.cot, bf16[384,1536]{1,0:T(8,128)(2,1)} %collective-permute-done.26.up, ...), custom_call_target="tpu_custom_call" | custom-call | flops 301989888 | bytes 6193152 | tf_op jit(solution)/shard_map/pallas_call | solution.py:256
  165.0 1.8 collective-permute-start.30
  166.8 8.5 %collective-permute-done.34 = bf16[96,1536]{1,0:T(8,128)(2,1)S(1)} collective-permute-done((bf16[96,1536]{1,0:T(8,128)(2,1)S(1)}, bf16[96,1536]{1,0:T(8,128)(2,1)S(1)}, u32[]{:S(2)}, u32[]{:S(2)}) %collective-permute-start.34) | collective-permute-done | bytes 294944 | tf_op jit(solution)/shard_map/ppermute | solution.py:65
  177.1 3.3 %collective-permute-start.25 = (f32[768,128]{1,0:T(8,128)S(1)}, f32[768,128]{1,0:T(8,128)S(1)}, u32[]{:S(2)}, u32[]{:S(2)}) collective-permute-start(f32[768,128]{1,0:T(8,128)S(1)} %get-tuple-element.88), channel_id=1, source_target_pairs={{0,3},{1,0},{2,1},{3,2},{4,7},{5,4},{6,5},{7,6},{8,11},{9,8},{10,9... | collective-permute-start | bytes 1179656 | tf_op jit(solution)/shard_map/ppermute | solution.py:65
  180.4 1.1 maximum_select_fusion
  181.6 3.4 %shard_map.231 = (f32[6,12,3072]{2,1,0:T(8,128)}, f32[6,12,3072]{2,1,0:T(8,128)}, f32[6,12,3072]{2,1,0:T(8,128)}) custom-call(f32[48,3072]{1,0:T(8,128)S(1)} %maximum_select_fusion.1.wgrad, bf16[48,3072]{1,0:T(8,128)(2,1)S(1)} %copy-done.13, f32[6,12,3072]{2,1,0:T(8,128)S(1)} %copy-done.17, f32[6,12,3072]{2,1,0:T(8,128)S(1)} %copy-done.7, ...), custom_call_target="tpu_custom_call" | custom-call | flops 8000000 | bytes 7000000 | tf_op jit(solution)/shard_map/pallas_call | solution.py:151
  185.0 4.6 %collective-permute-done.23 = f32[768,128]{1,0:T(8,128)S(1)} collective-permute-done((f32[768,128]{1,0:T(8,128)S(1)}, f32[768,128]{1,0:T(8,128)S(1)}, u32[]{:S(2)}, u32[]{:S(2)}) %collective-permute-start.23) | collective-permute-done | bytes 393248 | tf_op jit(solution)/shard_map/ppermute | solution.py:65
  189.6 10.5 %collective-permute-done.25 = f32[768,128]{1,0:T(8,128)S(1)} collective-permute-done((f32[768,128]{1,0:T(8,128)S(1)}, f32[768,128]{1,0:T(8,128)S(1)}, u32[]{:S(2)}, u32[]{:S(2)}) %collective-permute-start.25) | collective-permute-done | bytes 393248 | tf_op jit(solution)/shard_map/ppermute | solution.py:65
  200.1 10.8 %collective-permute-done.24 = f32[768,128]{1,0:T(8,128)S(1)} collective-permute-done((f32[768,128]{1,0:T(8,128)S(1)}, f32[768,128]{1,0:T(8,128)S(1)}, u32[]{:S(2)}, u32[]{:S(2)}) %collective-permute-start.24) | collective-permute-done | bytes 393248 | tf_op jit(solution)/shard_map/ppermute | solution.py:65
  (127 shorter events, 16.2 us)
Async XLA Ops:
  4.0 8.7 %copy-start.26 = (bf16[128,768]{1,0:T(8,128)(2,1)S(1)}, bf16[128,768]{1,0:T(8,128)(2,1)}, u32[]{:S(2)}) copy-start(bf16[128,768]{1,0:T(8,128)(2,1)} %param.19) | copy-start | bytes 589828
  4.0 15.7 %copy-start.25 = (bf16[128,3072]{1,0:T(8,128)(2,1)S(1)}, bf16[128,3072]{1,0:T(8,128)(2,1)}, u32[]{:S(2)}) copy-start(bf16[128,3072]{1,0:T(8,128)(2,1)} %param.23) | copy-start | bytes 2359300
  4.9 4.3 %collective-permute-start.5 = (bf16[48,1536]{1,0:T(8,128)(2,1)S(1)}, bf16[48,1536]{1,0:T(8,128)(2,1)S(1)}, u32[]{:S(2)}, u32[]{:S(2)}) collective-permute-start(bf16[48,1536]{1,0:T(8,128)(2,1)S(1)} %get-tuple-element.97), channel_id=1, source_target_pairs={{0,4},{1,5},{2,6},{3,7},{4,0},{5,1},{6,2},{7,3},{8,12},{9,13},{10,... | collective-permute-start | bytes 442376 | tf_op jit(solution)/shard_map/ppermute | solution.py:65
  9.3 10.3 %collective-permute-start.8 = (bf16[96,1536]{1,0:T(8,128)(2,1)S(1)}, bf16[96,1536]{1,0:T(8,128)(2,1)S(1)}, u32[]{:S(2)}, u32[]{:S(2)}) collective-permute-start(bf16[96,1536]{1,0:T(8,128)(2,1)S(1)} %pad_maximum_fusion.2.refs_0_), channel_id=1, source_target_pairs={{0,32},{1,33},{2,34},{3,35},{4,12},{5,13},{6,14},{7,15},{8,40},{9,... | collective-permute-start | bytes 884744 | tf_op jit(solution)/shard_map/ppermute | solution.py:65
  9.4 11.1 %collective-permute-start.7 = (bf16[96,1536]{1,0:T(8,128)(2,1)S(1)}, bf16[96,1536]{1,0:T(8,128)(2,1)S(1)}, u32[]{:S(2)}, u32[]{:S(2)}) collective-permute-start(bf16[96,1536]{1,0:T(8,128)(2,1)S(1)} %pad_maximum_fusion.2.refs_0_), channel_id=1, source_target_pairs={{0,64},{1,65},{2,66},{3,67},{4,20},{5,21},{6,22},{7,23},{8,72},{9,... | collective-permute-start | bytes 884744 | tf_op jit(solution)/shard_map/ppermute | solution.py:65
  11.6 8.9 %collective-permute-start.6 = (bf16[96,1536]{1,0:T(8,128)(2,1)S(1)}, bf16[96,1536]{1,0:T(8,128)(2,1)S(1)}, u32[]{:S(2)}, u32[]{:S(2)}) collective-permute-start(bf16[96,1536]{1,0:T(8,128)(2,1)S(1)} %pad_maximum_fusion.2.refs_0_), channel_id=1, source_target_pairs={{0,96},{1,97},{2,98},{3,99},{4,28},{5,29},{6,30},{7,31},{8,104},{9... | collective-permute-start | bytes 884744 | tf_op jit(solution)/shard_map/ppermute | solution.py:65
  12.8 11.5 %collective-permute-start.2 = (bf16[768,128]{1,0:T(8,128)(2,1)S(1)}, bf16[768,128]{1,0:T(8,128)(2,1)}, u32[]{:S(2)}, u32[]{:S(2)}) collective-permute-start(bf16[768,128]{1,0:T(8,128)(2,1)S(1)} %bitcast.13), channel_id=1, source_target_pairs={{0,3},{1,0},{2,1},{3,2},{4,7},{5,4},{6,5},{7,6},{8,11},{9,8},{10,9... | collective-permute-start | bytes 589832 | tf_op jit(solution)/shard_map/ppermute | solution.py:65
  17.2 16.2 %collective-permute-start.1 = (bf16[768,128]{1,0:T(8,128)(2,1)S(1)}, bf16[768,128]{1,0:T(8,128)(2,1)}, u32[]{:S(2)}, u32[]{:S(2)}) collective-permute-start(bf16[768,128]{1,0:T(8,128)(2,1)S(1)} %bitcast.14), channel_id=1, source_target_pairs={{0,2},{1,3},{2,0},{3,1},{4,6},{5,7},{6,4},{7,5},{8,10},{9,11},{10,... | collective-permute-start | bytes 589832 | tf_op jit(solution)/shard_map/ppermute | solution.py:65
  19.6 13.8 %collective-permute-start = (bf16[768,128]{1,0:T(8,128)(2,1)S(1)}, bf16[768,128]{1,0:T(8,128)(2,1)}, u32[]{:S(2)}, u32[]{:S(2)}) collective-permute-start(bf16[768,128]{1,0:T(8,128)(2,1)S(1)} %bitcast.15), channel_id=1, source_target_pairs={{0,1},{1,2},{2,3},{3,0},{4,5},{5,6},{6,7},{7,4},{8,9},{9,10},{10,1... | collective-permute-start | bytes 589832 | tf_op jit(solution)/shard_map/ppermute | solution.py:65
  20.4 15.4 %copy-start.27 = (s32[64]{0:T(128)S(1)}, s32[64]{0:T(128)}, u32[]{:S(2)}) copy-start(s32[64]{0:T(128)} %constant.161.clone) | copy-start | bytes 772
  20.4 15.4 %copy-start.28 = (s32[64]{0:T(128)S(1)}, s32[64]{0:T(128)}, u32[]{:S(2)}) copy-start(s32[64]{0:T(128)} %constant.160.clone) | copy-start | bytes 772
  20.4 15.4 %copy-start.29 = (s32[64]{0:T(128)S(1)}, s32[64]{0:T(128)}, u32[]{:S(2)}) copy-start(s32[64]{0:T(128)} %constant.159.clone) | copy-start | bytes 772
  20.4 15.4 %copy-start.30 = (s32[64]{0:T(128)S(1)}, s32[64]{0:T(128)}, u32[]{:S(2)}) copy-start(s32[64]{0:T(128)} %constant.158.clone) | copy-start | bytes 772
  20.4 15.4 %copy-start.31 = (s32[64]{0:T(128)S(1)}, s32[64]{0:T(128)}, u32[]{:S(2)}) copy-start(s32[64]{0:T(128)} %constant.157.clone) | copy-start | bytes 772
  20.4 15.4 %copy-start.32 = (s32[64]{0:T(128)S(1)}, s32[64]{0:T(128)}, u32[]{:S(2)}) copy-start(s32[64]{0:T(128)} %constant.156.clone) | copy-start | bytes 772
  21.6 19.0 %collective-permute-start.10 = (bf16[384,1536]{1,0:T(8,128)(2,1)}, bf16[384,1536]{1,0:T(8,128)(2,1)}, u32[]{:S(2)}, u32[]{:S(2)}) collective-permute-start(bf16[384,1536]{1,0:T(8,128)(2,1)} %shard_map.220.refs_0_), channel_id=1, source_target_pairs={{0,8},{1,9},{2,10},{3,11},{4,36},{5,37},{6,38},{7,39},{8,16},{9,17... | collective-permute-start | bytes 3538952 | tf_op jit(solution)/shard_map/ppermute | solution.py:65
  21.6 19.0 %collective-permute-start.9 = (bf16[384,1536]{1,0:T(8,128)(2,1)}, bf16[384,1536]{1,0:T(8,128)(2,1)}, u32[]{:S(2)}, u32[]{:S(2)}) collective-permute-start(bf16[384,1536]{1,0:T(8,128)(2,1)} %shard_map.220.refs_0_), channel_id=1, source_target_pairs={{0,24},{1,25},{2,26},{3,27},{4,100},{5,101},{6,102},{7,103},{8,0},... | collective-permute-start | bytes 3538952 | tf_op jit(solution)/shard_map/ppermute | solution.py:65
  24.3 12.4 %collective-permute-start.4 = (bf16[128,1536]{1,0:T(8,128)(2,1)}, bf16[128,1536]{1,0:T(8,128)(2,1)}, u32[]{:S(2)}, u32[]{:S(2)}) collective-permute-start(bf16[128,1536]{1,0:T(8,128)(2,1)} %get-tuple-element.93), channel_id=1, source_target_pairs={{0,4},{1,5},{2,6},{3,7},{4,0},{5,1},{6,2},{7,3},{8,12},{9,13},{10,... | collective-permute-start | bytes 1179656 | tf_op jit(solution)/shard_map/ppermute | solution.py:65
  34.5 3.2 %collective-permute-start.3 = (bf16[3072,128]{1,0:T(8,128)(2,1)S(1)}, bf16[3072,128]{1,0:T(8,128)(2,1)S(1)}, u32[]{:S(2)}, u32[]{:S(2)}) collective-permute-start(bf16[3072,128]{1,0:T(8,128)(2,1)S(1)} %pad_maximum_fusion.mine), channel_id=1, source_target_pairs={{0,4},{1,5},{2,6},{3,7},{4,0},{5,1},{6,2},{7,3},{8,12},{9,13},{10,... | collective-permute-start | bytes 2359304 | tf_op jit(solution)/shard_map/ppermute | solution.py:65
  42.8 26.6 %collective-permute-start.11 = (bf16[384,1536]{1,0:T(8,128)(2,1)S(1)}, bf16[384,1536]{1,0:T(8,128)(2,1)S(1)}, u32[]{:S(2)}, u32[]{:S(2)}) collective-permute-start(bf16[384,1536]{1,0:T(8,128)(2,1)S(1)} %get-tuple-element.42), channel_id=1, source_target_pairs={{0,24},{1,25},{2,26},{3,27},{4,100},{5,101},{6,102},{7,103},{8,0},... | collective-permute-start | bytes 3538952 | tf_op jit(solution)/shard_map/ppermute | solution.py:65
  43.8 25.6 %collective-permute-start.12 = (bf16[384,1536]{1,0:T(8,128)(2,1)S(1)}, bf16[384,1536]{1,0:T(8,128)(2,1)S(1)}, u32[]{:S(2)}, u32[]{:S(2)}) collective-permute-start(bf16[384,1536]{1,0:T(8,128)(2,1)S(1)} %get-tuple-element.43), channel_id=1, source_target_pairs={{0,8},{1,9},{2,10},{3,11},{4,36},{5,37},{6,38},{7,39},{8,16},{9,17... | collective-permute-start | bytes 3538952 | tf_op jit(solution)/shard_map/ppermute | solution.py:65
  44.4 11.6 %collective-permute-start.13 = (bf16[96,1536]{1,0:T(8,128)(2,1)S(1)}, bf16[96,1536]{1,0:T(8,128)(2,1)S(1)}, u32[]{:S(2)}, u32[]{:S(2)}) collective-permute-start(bf16[96,1536]{1,0:T(8,128)(2,1)S(1)} %pad_maximum_fusion.2.refs_0_), channel_id=1, source_target_pairs={{0,128},{1,129},{2,130},{3,131},{4,132},{5,133},{6,134},{7,135},{8... | collective-permute-start | bytes 884744 | tf_op jit(solution)/shard_map/ppermute | solution.py:65
  56.0 13.4 %collective-permute-start.16 = (bf16[96,1536]{1,0:T(8,128)(2,1)S(1)}, bf16[96,1536]{1,0:T(8,128)(2,1)S(1)}, u32[]{:S(2)}, u32[]{:S(2)}) collective-permute-start(bf16[96,1536]{1,0:T(8,128)(2,1)S(1)} %collective-permute-done.13.refs_0_), channel_id=1, source_target_pairs={{0,32},{1,33},{2,34},{3,35},{4,12},{5,13},{6,14},{7,15},{8,40},{9,... | collective-permute-start | bytes 884744 | tf_op jit(solution)/shard_map/ppermute | solution.py:65
  57.5 11.8 %collective-permute-start.15 = (bf16[96,1536]{1,0:T(8,128)(2,1)S(1)}, bf16[96,1536]{1,0:T(8,128)(2,1)S(1)}, u32[]{:S(2)}, u32[]{:S(2)}) collective-permute-start(bf16[96,1536]{1,0:T(8,128)(2,1)S(1)} %collective-permute-done.13.refs_0_), channel_id=1, source_target_pairs={{0,64},{1,65},{2,66},{3,67},{4,20},{5,21},{6,22},{7,23},{8,72},{9,... | collective-permute-start | bytes 884744 | tf_op jit(solution)/shard_map/ppermute | solution.py:65
  57.5 11.8 %collective-permute-start.14 = (bf16[96,1536]{1,0:T(8,128)(2,1)S(1)}, bf16[96,1536]{1,0:T(8,128)(2,1)S(1)}, u32[]{:S(2)}, u32[]{:S(2)}) collective-permute-start(bf16[96,1536]{1,0:T(8,128)(2,1)S(1)} %collective-permute-done.13.refs_0_), channel_id=1, source_target_pairs={{0,96},{1,97},{2,98},{3,99},{4,28},{5,29},{6,30},{7,31},{8,104},{9... | collective-permute-start | bytes 884744 | tf_op jit(solution)/shard_map/ppermute | solution.py:65
  70.8 29.8 %collective-permute-start.17 = (bf16[768,1536]{1,0:T(8,128)(2,1)S(1)}, bf16[768,1536]{1,0:T(8,128)(2,1)S(1)}, u32[]{:S(2)}, u32[]{:S(2)}) collective-permute-start(bf16[768,1536]{1,0:T(8,128)(2,1)S(1)} %get-tuple-element.46), channel_id=1, source_target_pairs={{0,24},{1,25},{2,26},{3,27},{4,100},{5,101},{6,102},{7,103},{8,0},... | collective-permute-start | bytes 7077896 | tf_op jit(solution)/shard_map/ppermute | solution.py:65
  73.1 29.2 %collective-permute-start.18 = (bf16[768,1536]{1,0:T(8,128)(2,1)S(1)}, bf16[768,1536]{1,0:T(8,128)(2,1)S(1)}, u32[]{:S(2)}, u32[]{:S(2)}) collective-permute-start(bf16[768,1536]{1,0:T(8,128)(2,1)S(1)} %get-tuple-element.45.refs_1_), channel_id=1, source_target_pairs={{0,8},{1,9},{2,10},{3,11},{4,36},{5,37},{6,38},{7,39},{8,16},{9,17... | collective-permute-start | bytes 7077896 | tf_op jit(solution)/shard_map/ppermute | solution.py:65
  103.7 15.3 %collective-permute-start.19 = (bf16[384,1536]{1,0:T(8,128)(2,1)S(1)}, bf16[384,1536]{1,0:T(8,128)(2,1)S(1)}, u32[]{:S(2)}, u32[]{:S(2)}) collective-permute-start(bf16[384,1536]{1,0:T(8,128)(2,1)S(1)} %get-tuple-element.48), channel_id=1, source_target_pairs={{0,24},{1,25},{2,26},{3,27},{4,100},{5,101},{6,102},{7,103},{8,0},... | collective-permute-start | bytes 3538952 | tf_op jit(solution)/shard_map/ppermute | solution.py:65
  105.1 16.6 %collective-permute-start.20 = (bf16[384,1536]{1,0:T(8,128)(2,1)S(1)}, bf16[384,1536]{1,0:T(8,128)(2,1)S(1)}, u32[]{:S(2)}, u32[]{:S(2)}) collective-permute-start(bf16[384,1536]{1,0:T(8,128)(2,1)S(1)} %get-tuple-element.49), channel_id=1, source_target_pairs={{0,8},{1,9},{2,10},{3,11},{4,36},{5,37},{6,38},{7,39},{8,16},{9,17... | collective-permute-start | bytes 3538952 | tf_op jit(solution)/shard_map/ppermute | solution.py:65
  123.7 38.0 %collective-permute-start.26 = (bf16[384,1536]{1,0:T(8,128)(2,1)}, bf16[384,1536]{1,0:T(8,128)(2,1)}, u32[]{:S(2)}, u32[]{:S(2)}) collective-permute-start(bf16[384,1536]{1,0:T(8,128)(2,1)} %get-tuple-element.63), channel_id=1, source_target_pairs={{0,8},{1,9},{2,10},{3,11},{4,36},{5,37},{6,38},{7,39},{8,16},{9,17... | collective-permute-start | bytes 3538952 | tf_op jit(solution)/shard_map/ppermute | solution.py:65
  123.8 38.0 %collective-permute-start.27 = (bf16[384,1536]{1,0:T(8,128)(2,1)}, bf16[384,1536]{1,0:T(8,128)(2,1)}, u32[]{:S(2)}, u32[]{:S(2)}) collective-permute-start(bf16[384,1536]{1,0:T(8,128)(2,1)} %get-tuple-element.64), channel_id=1, source_target_pairs={{0,24},{1,25},{2,26},{3,27},{4,100},{5,101},{6,102},{7,103},{8,0},... | collective-permute-start | bytes 3538952 | tf_op jit(solution)/shard_map/ppermute | solution.py:65
  130.4 12.3 %collective-permute-start.31 = (bf16[96,1536]{1,0:T(8,128)(2,1)S(1)}, bf16[96,1536]{1,0:T(8,128)(2,1)S(1)}, u32[]{:S(2)}, u32[]{:S(2)}) collective-permute-start(bf16[96,1536]{1,0:T(8,128)(2,1)S(1)} %get-tuple-element.70), channel_id=1, source_target_pairs={{0,32},{1,33},{2,34},{3,35},{4,12},{5,13},{6,14},{7,15},{8,40},{9,... | collective-permute-start | bytes 884744 | tf_op jit(solution)/shard_map/ppermute | solution.py:65
  130.7 24.4 %collective-permute-start.32 = (bf16[96,1536]{1,0:T(8,128)(2,1)S(1)}, bf16[96,1536]{1,0:T(8,128)(2,1)S(1)}, u32[]{:S(2)}, u32[]{:S(2)}) collective-permute-start(bf16[96,1536]{1,0:T(8,128)(2,1)S(1)} %get-tuple-element.71), channel_id=1, source_target_pairs={{0,64},{1,65},{2,66},{3,67},{4,20},{5,21},{6,22},{7,23},{8,72},{9,... | collective-permute-start | bytes 884744 | tf_op jit(solution)/shard_map/ppermute | solution.py:65
  132.7 22.4 %collective-permute-start.33 = (bf16[96,1536]{1,0:T(8,128)(2,1)S(1)}, bf16[96,1536]{1,0:T(8,128)(2,1)S(1)}, u32[]{:S(2)}, u32[]{:S(2)}) collective-permute-start(bf16[96,1536]{1,0:T(8,128)(2,1)S(1)} %get-tuple-element.72), channel_id=1, source_target_pairs={{0,96},{1,97},{2,98},{3,99},{4,28},{5,29},{6,30},{7,31},{8,104},{9... | collective-permute-start | bytes 884744 | tf_op jit(solution)/shard_map/ppermute | solution.py:65
  133.2 5.3 %copy-start.2 = (bf16[768,1536]{1,0:T(8,128)(2,1)S(1)}, bf16[768,1536]{1,0:T(8,128)(2,1)}, u32[]{:S(2)}) copy-start(bf16[768,1536]{1,0:T(8,128)(2,1)} %copy-done) | copy-start | bytes 7077892
  133.2 5.3 %copy-start.5 = (bf16[768,1536]{1,0:T(8,128)(2,1)S(1)}, bf16[768,1536]{1,0:T(8,128)(2,1)}, u32[]{:S(2)}) copy-start(bf16[768,1536]{1,0:T(8,128)(2,1)} %copy-done.3) | copy-start | bytes 7077892
  133.2 5.3 %copy-start.11 = (bf16[768,1536]{1,0:T(8,128)(2,1)S(1)}, bf16[768,1536]{1,0:T(8,128)(2,1)}, u32[]{:S(2)}) copy-start(bf16[768,1536]{1,0:T(8,128)(2,1)} %copy-done.10) | copy-start | bytes 7077892
  142.7 34.0 %collective-permute-start.22 = (f32[3072,128]{1,0:T(8,128)S(1)}, f32[3072,128]{1,0:T(8,128)S(1)}, u32[]{:S(2)}, u32[]{:S(2)}) collective-permute-start(f32[3072,128]{1,0:T(8,128)S(1)} %get-tuple-element.62), channel_id=1, source_target_pairs={{0,4},{1,5},{2,6},{3,7},{4,0},{5,1},{6,2},{7,3},{8,12},{9,13},{10,... | collective-permute-start | bytes 4718600 | tf_op jit(solution)/shard_map/ppermute | solution.py:65
  155.2 20.1 %collective-permute-start.34 = (bf16[96,1536]{1,0:T(8,128)(2,1)S(1)}, bf16[96,1536]{1,0:T(8,128)(2,1)S(1)}, u32[]{:S(2)}, u32[]{:S(2)}) collective-permute-start(bf16[96,1536]{1,0:T(8,128)(2,1)S(1)} %add_convert_fusion), channel_id=1, source_target_pairs={{0,128},{1,129},{2,130},{3,131},{4,132},{5,133},{6,134},{7,135},{8... | collective-permute-start | bytes 884744 | tf_op jit(solution)/shard_map/ppermute | solution.py:65
  164.0 12.0 %collective-permute-start.28 = (bf16[96,1536]{1,0:T(8,128)(2,1)S(1)}, bf16[96,1536]{1,0:T(8,128)(2,1)S(1)}, u32[]{:S(2)}, u32[]{:S(2)}) collective-permute-start(bf16[96,1536]{1,0:T(8,128)(2,1)S(1)} %get-tuple-element.66), channel_id=1, source_target_pairs={{0,32},{1,33},{2,34},{3,35},{4,12},{5,13},{6,14},{7,15},{8,40},{9,... | collective-permute-start | bytes 884744 | tf_op jit(solution)/shard_map/ppermute | solution.py:65
  164.1 11.9 %collective-permute-start.29 = (bf16[96,1536]{1,0:T(8,128)(2,1)S(1)}, bf16[96,1536]{1,0:T(8,128)(2,1)S(1)}, u32[]{:S(2)}, u32[]{:S(2)}) collective-permute-start(bf16[96,1536]{1,0:T(8,128)(2,1)S(1)} %get-tuple-element.67), channel_id=1, source_target_pairs={{0,64},{1,65},{2,66},{3,67},{4,20},{5,21},{6,22},{7,23},{8,72},{9,... | collective-permute-start | bytes 884744 | tf_op jit(solution)/shard_map/ppermute | solution.py:65
  165.0 11.0 %collective-permute-start.30 = (bf16[96,1536]{1,0:T(8,128)(2,1)S(1)}, bf16[96,1536]{1,0:T(8,128)(2,1)S(1)}, u32[]{:S(2)}, u32[]{:S(2)}) collective-permute-start(bf16[96,1536]{1,0:T(8,128)(2,1)S(1)} %get-tuple-element.68), channel_id=1, source_target_pairs={{0,96},{1,97},{2,98},{3,99},{4,28},{5,29},{6,30},{7,31},{8,104},{9... | collective-permute-start | bytes 884744 | tf_op jit(solution)/shard_map/ppermute | solution.py:65
  175.3 5.1 %collective-permute-start.21 = (bf16[128,1536]{1,0:T(8,128)(2,1)S(1)}, bf16[128,1536]{1,0:T(8,128)(2,1)S(1)}, u32[]{:S(2)}, u32[]{:S(2)}) collective-permute-start(bf16[128,1536]{1,0:T(8,128)(2,1)S(1)} %get-tuple-element.91), channel_id=1, source_target_pairs={{0,4},{1,5},{2,6},{3,7},{4,0},{5,1},{6,2},{7,3},{8,12},{9,13},{10,... | collective-permute-start | bytes 1179656 | tf_op jit(solution)/shard_map/ppermute | solution.py:65
  176.2 5.3 %collective-permute-start.35 = (f32[48,1536]{1,0:T(8,128)S(1)}, f32[48,1536]{1,0:T(8,128)S(1)}, u32[]{:S(2)}, u32[]{:S(2)}) collective-permute-start(f32[48,1536]{1,0:T(8,128)S(1)} %get-tuple-element.95), channel_id=1, source_target_pairs={{0,4},{1,5},{2,6},{3,7},{4,0},{5,1},{6,2},{7,3},{8,12},{9,13},{10,... | collective-permute-start | bytes 884744 | tf_op jit(solution)/shard_map/ppermute | solution.py:65
  176.9 4.6 %copy-start.15 = (f32[6,12,3072]{2,1,0:T(8,128)S(1)}, f32[6,12,3072]{2,1,0:T(8,128)}, u32[]{:S(2)}) copy-start(f32[6,12,3072]{2,1,0:T(8,128)} %two.1) | copy-start | bytes 2654212
  177.0 12.6 %collective-permute-start.23 = (f32[768,128]{1,0:T(8,128)S(1)}, f32[768,128]{1,0:T(8,128)S(1)}, u32[]{:S(2)}, u32[]{:S(2)}) collective-permute-start(f32[768,128]{1,0:T(8,128)S(1)} %get-tuple-element.87), channel_id=1, source_target_pairs={{0,1},{1,2},{2,3},{3,0},{4,5},{5,6},{6,7},{7,4},{8,9},{9,10},{10,1... | collective-permute-start | bytes 1179656 | tf_op jit(solution)/shard_map/ppermute | solution.py:65
  177.1 23.0 %collective-permute-start.25 = (f32[768,128]{1,0:T(8,128)S(1)}, f32[768,128]{1,0:T(8,128)S(1)}, u32[]{:S(2)}, u32[]{:S(2)}) collective-permute-start(f32[768,128]{1,0:T(8,128)S(1)} %get-tuple-element.88), channel_id=1, source_target_pairs={{0,3},{1,0},{2,1},{3,2},{4,7},{5,4},{6,5},{7,6},{8,11},{9,8},{10,9... | collective-permute-start | bytes 1179656 | tf_op jit(solution)/shard_map/ppermute | solution.py:65
  180.4 30.5 %collective-permute-start.24 = (f32[768,128]{1,0:T(8,128)S(1)}, f32[768,128]{1,0:T(8,128)S(1)}, u32[]{:S(2)}, u32[]{:S(2)}) collective-permute-start(f32[768,128]{1,0:T(8,128)S(1)} %get-tuple-element.89), channel_id=1, source_target_pairs={{0,2},{1,3},{2,0},{3,1},{4,6},{5,7},{6,4},{7,5},{8,10},{9,11},{10,... | collective-permute-start | bytes 1179656 | tf_op jit(solution)/shard_map/ppermute | solution.py:65
  (21 other events, 50.2 us)
where the time goes:
time: 212 us
  waiting for transfers between devices  105 us (50%)
  starting transfers between devices  63.3 us (30%)
  Pallas kernels  24.4 us (12%)
  local copies, waits for them, and re-layouts  14.1 us (7%)
  other arithmetic  4.07 us (2%)
    ppermute x36, waiting for transfers between devices, send(): return lax.ppermute(value, AXES, pairs)  105 us
    ppermute x36, starting transfers between devices, send(): return lax.ppermute(value, AXES, pairs)  63.3 us
    pallas_call x10, Pallas kernels, in_vmem(): pl.pallas_call(kernel, in_specs=[IN_VMEM] * len(args), out_specs=[IN_VMEM...  18.5 us
    unnamed x68, local copies, waits for them, and re-layouts  12.3 us
  transfers between devices with their start and end apart: 36, of which 13 were waited for; matrix products, arithmetic and copies ran while one was open for 3% of the time, Pallas kernels for 8%

commit v1 on v0

--- a/solution.py
+++ b/solution.py
@@ -1,5 +1,4 @@
 import functools
-import math
 
 import jax
 import jax.numpy as jnp
@@ -27,6 +26,7 @@
 TILE = 512
 MIB = 1 << 20
 IN_VMEM = pl.BlockSpec(memory_space=pltpu.VMEM)
+LIGHT = pl.CostEstimate(flops=0, bytes_accessed=1, transcendentals=0)
 
 
 def pairs_of(target):
@@ -59,6 +59,10 @@
 
 def around(by):
     return pairs_of(lambda z, x, y, c, m: (z, x, y, c, m + by))
+
+
+def crossed(by):
+    return pairs_of(lambda z, x, y, c, m: (z, x, y, c, m ^ by))
 
 
 def send(value, pairs):
@@ -109,7 +113,7 @@
         ],
         scratch_shapes=[pltpu.VMEM((wide // 128 * ROWS, 128), F32)],
         compiler_params=pltpu.CompilerParams(vmem_limit_bytes=16 * MIB),
-        cost_estimate=pl.CostEstimate(flops=8000000, bytes_accessed=2800000, transcendentals=221184),
+        cost_estimate=LIGHT,
     )(logits, gumbel, weight)
 
 
@@ -156,7 +160,7 @@
         out_shape=[out, out, out],
         scratch_shapes=[pltpu.VMEM((wide // 128 * ROWS, 128), F32)],
         compiler_params=pltpu.CompilerParams(vmem_limit_bytes=16 * MIB),
-        cost_estimate=pl.CostEstimate(flops=8000000, bytes_accessed=7000000, transcendentals=221184),
+        cost_estimate=LIGHT,
     )(wgrad, weight, probs, logits, one, two)
 
 
@@ -174,7 +178,7 @@
         out_specs=IN_VMEM,
         out_shape=jax.ShapeDtypeStruct((3072, 256), BF16),
         compiler_params=pltpu.CompilerParams(vmem_limit_bytes=16 * MIB),
-        cost_estimate=pl.CostEstimate(flops=0, bytes_accessed=3200000, transcendentals=0),
+        cost_estimate=LIGHT,
     )(place, mine, other)
 
 
@@ -197,7 +201,7 @@
         out_specs=[IN_VMEM] * 2,
         out_shape=[out, out],
         compiler_params=pltpu.CompilerParams(vmem_limit_bytes=16 * MIB),
-        cost_estimate=pl.CostEstimate(flops=0, bytes_accessed=6400000, transcendentals=0),
+        cost_estimate=LIGHT,
     )(place, *pieces)
 
 
@@ -211,37 +215,44 @@
         out[i * 96 : (i + 1) * 96, :] = ref[...]
 
 
-def lead_kernel(start, acts, cot, near, far, up, down):
+def lead(acts, cot, start, base, up, down):
+    for at in range(0, HALF, TILE):
+        cols = slice(at, at + TILE)
+        up[base : base + 192, cols] = share(acts, cot, start, 192, at).astype(BF16)
+        down[base : base + 192, cols] = share(acts, cot, start + 192, 192, at).astype(BF16)
+
+
+def follow(acts, cot, start_up, start_down, low, high, base, up, down):
+    for at in range(0, HALF, TILE):
+        cols = slice(at, at + TILE)
+        got = share(acts, cot, start_up, 192, at) + low[base : base + 192, cols].astype(F32)
+        up[:192, cols] = got.astype(BF16)
+        up[192:384, cols] = share(acts, cot, start_up + 192, 192, at).astype(BF16)
+        down[:192, cols] = share(acts, cot, start_down, 192, at).astype(BF16)
+        got = share(acts, cot, start_down + 192, 192, at) + high[base : base + 192, cols].astype(F32)
+        down[192:384, cols] = got.astype(BF16)
+
+
+def second_kernel(start, acts, cot, near, far, up, down):
     up[:192, :] = far[192:384, :]
     down[:192, :] = near[:192, :]
-    for at in range(0, HALF, TILE):
-        cols = slice(at, at + TILE)
-        up[192:, cols] = share(acts, cot, start, 192, at).astype(BF16)
-        down[192:, cols] = share(acts, cot, start + 192, 192, at).astype(BF16)
-
-
-def follow_kernel(start_up, start_down, acts, cot, low, high, *refs):
-    up, down = refs[-2:]
-    base = 96 * (len(refs) - 2)
-    for i, ref in enumerate(refs[:-2]):
-        up[i * 96 : (i + 1) * 96, :] = ref[...]
-        down[i * 96 : (i + 1) * 96, :] = ref[...]
-    for at in range(0, HALF, TILE):
-        cols = slice(at, at + TILE)
-        got = share(acts, cot, start_up, 192, at) + low[192:, cols].astype(F32)
-        up[base : base + 192, cols] = got.astype(BF16)
-        up[base + 192 :, cols] = share(acts, cot, start_up + 192, 192, at).astype(BF16)
-        down[base : base + 192, cols] = share(acts, cot, start_down, 192, at).astype(BF16)
-        got = share(acts, cot, start_down + 192, 192, at) + high[192:, cols].astype(F32)
-        down[base + 192 :, cols] = got.astype(BF16)
+    lead(acts, cot, start, 192, up, down)
+
+
+def third_kernel(start_up, start_down, acts, cot, low, high, up, down):
+    follow(acts, cot, start_up, start_down, low, high, 192, up, down)
+
+
+def sum_kernel(own, one, two, three, out):
+    total = own[...] + one[...].astype(F32) + two[...].astype(F32) + three[...].astype(F32)
+    out[...] = total.astype(out.dtype)
 
 
 def keep_kernel(start, acts, cot, up, down, own, *others):
-    base = up.shape[0] - 384
     for at in range(0, HALF, TILE):
         cols = slice(at, at + TILE)
         for i in range(4):
-            rows = slice(base + i * 96, base + i * 96 + 96)
+            rows = slice(i * 96, i * 96 + 96)
             got = share(acts, cot, start + i * 96, 96, at)
             got = got + up[rows, cols].astype(F32) + down[rows, cols].astype(F32)
             if i == 0:
@@ -250,16 +261,21 @@
                 others[i - 1][:, cols] = got.astype(BF16)
 
 
-def in_vmem(kernel, out_shape, flops, *args):
-    moved = sum(a.size * a.dtype.itemsize for a in args)
-    moved += sum(math.prod(o.shape) * o.dtype.itemsize for o in out_shape)
+def in_vmem(kernel, out_shape, *args, after=()):
+    if after:
+        inner, count, kept = kernel, len(args), len(args) + len(after)
+
+        def kernel(*refs):
+            inner(*refs[:count], *refs[kept:])
+
+        args = args + tuple(after)
     return pl.pallas_call(
         kernel,
         in_specs=[IN_VMEM] * len(args),
         out_specs=[IN_VMEM] * len(out_shape),
         out_shape=out_shape,
         compiler_params=pltpu.CompilerParams(vmem_limit_bytes=24 * MIB),
-        cost_estimate=pl.CostEstimate(flops=flops, bytes_accessed=moved, transcendentals=0),
+        cost_estimate=LIGHT,
     )(*args)
 
 
@@ -267,30 +283,32 @@
     return jax.ShapeDtypeStruct((rows, HALF), BF16)
 
 
-def product_kernel(starts, counts, first, acts, cot, *refs):
-    size = len(starts)
+def product_kernel(spans, first, acts, cot, *refs):
+    size = len(spans)
     before = None if first else refs[0]
     refs = refs if first else refs[1:]
     pieces, result, grads = refs[:size], refs[size], refs[size + 1 :]
     for at in range(0, HALF, TILE):
         cols = slice(at, at + TILE)
         total = None if first else before[:, cols]
-        for start, count, piece in zip(starts, counts, pieces):
-            term = dot(acts[start : start + count, :], piece[:count, cols], ((0,), (0,)))
+        for (start, skip, count), piece in zip(spans, pieces):
+            rows = piece[skip : skip + count, cols]
+            term = dot(acts[start : start + count, :], rows, ((0,), (0,)))
             total = term if total is None else total + term
         result[:, cols] = total
-    for count, piece, grad in zip(counts, pieces, grads):
-        grad[...] = dot(piece[:count, :], cot[...], ((1,), (1,)))
-
-
-def products(acts, cot, before, starts, counts, pieces):
+    for (start, skip, count), piece, grad in zip(spans, pieces, grads):
+        grad[...] = dot(piece[skip : skip + count, :], cot[...], ((1,), (1,)))
+
+
+def products(acts, cot, before, parts):
     first = before is None
+    spans = [p[:3] for p in parts]
     shapes = [jax.ShapeDtypeStruct((256, HALF), F32)]
-    shapes += [jax.ShapeDtypeStruct((n, 256), F32) for n in counts]
-    args = [acts, cot] + ([] if first else [before]) + pieces
+    shapes += [jax.ShapeDtypeStruct((p[2], 256), F32) for p in parts]
+    args = [acts, cot] + ([] if first else [before]) + [p[3] for p in parts]
     return in_vmem(
-        functools.partial(product_kernel, starts, counts, first),
-        shapes, 4 * sum(counts) * 256 * HALF, *args
+        functools.partial(product_kernel, spans, first),
+        shapes, *args
     )
 
 
@@ -317,53 +335,87 @@
     block = jnp.concatenate([half(masked, core), send(half(masked, 1 - core), SIBLING)], axis=0)
     blocks = [block, send(block, PARTNER)]
 
+    def start_of(dz, db):
+        return (dz * 4 + db) * 384
+
+    def spread_a(mine):
+        return [mine, send(mine, A_DOWN), send(mine, A_TWO), send(mine, A_UP)]
+
+    def kept(dz, up, down, after):
+        own, one, two, three = in_vmem(
+            functools.partial(keep_kernel, start_of(dz, 0)),
+            [jax.ShapeDtypeStruct((96, HALF), F32)] + [shape16(96)] * 3, acts, cot, up, down,
+            after=after,
+        )
+        return own, send(one, A_UP), send(two, A_TWO), send(three, A_DOWN)
+
     flipped = tokens.T
-    own = jnp.concatenate([flipped] + [send(flipped, around(r)) for r in (1, 2, 3)], axis=0)
-    others = send(own, SIBLING)
-    came = jnp.concatenate([((mp - r) % 4) * 16 + np.arange(16) for r in range(4)])
-    acts = meet(met_at[came], own, others)
+    own = jnp.concatenate([flipped, send(flipped, crossed(1))], axis=0)
+    whole_x = jnp.concatenate([own, send(own, crossed(2))], axis=0)
+
+    line0 = in_vmem(
+        line_kernel, [shape16(384)], *spread_a(blocks[0]), after=(blocks[1], own)
+    )[0]
+    near0, far0 = send(line0, B_DOWN), send(line0, B_UP)
+    line1 = in_vmem(line_kernel, [shape16(384)], *spread_a(blocks[1]), after=(whole_x,))[0]
+    near1, far1 = send(line1, B_DOWN), send(line1, B_UP)
+
+    came = jnp.concatenate([(mp ^ r) * 16 + np.arange(16) for r in range(4)])
+    acts = meet(met_at[came], whole_x, send(whole_x, SIBLING))
     cot = jnp.concatenate(
         [half(cotangent, core), send(half(cotangent, 1 - core), SIBLING)], axis=0
     )
 
-    def start_of(dz, db):
-        return (dz * 4 + db) * 384
-
-    def spread_a(mine):
-        return [mine, send(mine, A_DOWN), send(mine, A_TWO), send(mine, A_UP)]
-
-    def kept(dz, up, down):
-        own, one, two, three = in_vmem(
-            functools.partial(keep_kernel, start_of(dz, 0)),
-            [jax.ShapeDtypeStruct((96, HALF), F32)] + [shape16(96)] * 3, work, acts, cot, up, down,
-        )
-        one, two, three = send(one, A_UP), send(two, A_TWO), send(three, A_DOWN)
-        return own + one.astype(F32) + two.astype(F32) + three.astype(F32)
-
-    work = 2 * 384 * 256 * HALF
-    line0 = in_vmem(line_kernel, [shape16(384)], 0, *spread_a(blocks[0]))[0]
-    near0, far0 = send(line0, B_DOWN), send(line0, B_UP)
-    up, down = in_vmem(
-        functools.partial(lead_kernel, start_of(1, 2)), [shape16(384)] * 2, work, acts, cot, near0, far0
-    )
-    high0, low0 = send(up, B_UP), send(down, B_DOWN)
-    line1, down = in_vmem(
-        functools.partial(follow_kernel, start_of(1, 1), start_of(1, 3)),
-        [shape16(768)] * 2, 2 * work, acts, cot, high0, low0, *spread_a(blocks[1]),
-    )
-    far1, near1 = send(line1, B_UP), send(down, B_DOWN)
-    up, down = in_vmem(
-        functools.partial(lead_kernel, start_of(0, 2)), [shape16(384)] * 2, work, acts, cot, near1, far1
-    )
-    high1, low1 = send(up, B_UP), send(down, B_DOWN)
-    sums = {1: kept(1, far1, near1)}
-    up, down = in_vmem(
-        functools.partial(follow_kernel, start_of(0, 1), start_of(0, 3)),
-        [shape16(384)] * 2, 2 * work, acts, cot, high1, low1,
-    )
-    up, down = send(up, B_UP), send(down, B_DOWN)
-    sums[0] = kept(0, up, down)
-    wsum = sums[0] + send(sums[1].astype(BF16), PARTNER).astype(F32)
+    up2, down2 = in_vmem(
+        functools.partial(second_kernel, start_of(1, 2)),
+        [shape16(384)] * 2, acts, cot, near0, far0, after=(line1,),
+    )
+    high0, low0 = send(up2, B_UP), send(down2, B_DOWN)
+    up3, down3 = in_vmem(
+        functools.partial(second_kernel, start_of(0, 2)),
+        [shape16(384)] * 2, acts, cot, near1, far1, after=(up2,),
+    )
+    high1, low1 = send(up3, B_UP), send(down3, B_DOWN)
+    up4, down4 = in_vmem(
+        functools.partial(third_kernel, start_of(1, 1), start_of(1, 3)),
+        [shape16(384)] * 2, acts, cot, high0, low0, after=(up3,),
+    )
+    up4, down4 = send(up4, B_UP), send(down4, B_DOWN)
+    result, g0, g1, g3, g2, g4 = products(
+        acts, cot, None,
+        [
+            (start_of(0, 0), 0, 384, line0),
+            (start_of(0, 1), 0, 384, near0),
+            (start_of(0, 3), 0, 384, far0),
+            (start_of(0, 2), 0, 192, low0),
+            (start_of(0, 2) + 192, 0, 192, high0),
+        ],
+    )
+    up5, down5 = in_vmem(
+        functools.partial(third_kernel, start_of(0, 1), start_of(0, 3)),
+        [shape16(384)] * 2, acts, cot, high1, low1, after=(result,),
+    )
+    result, h0, h1, h3, h2, h4 = products(
+        acts, cot, result,
+        [
+            (start_of(1, 0), 0, 384, line1),
+            (start_of(1, 1), 0, 384, near1),
+            (start_of(1, 3), 0, 384, far1),
+            (start_of(1, 2), 0, 192, low1),
+            (start_of(1, 2) + 192, 0, 192, high1),
+        ],
+    )
+    up5, down5 = send(up5, B_UP), send(down5, B_DOWN)
+    mine, theirs = part(lies_at, [g0, g1, g2, g4, g3, h0, h1, h2, h4, h3])
+    grad = mine + send(theirs, SIBLING)
+    total = lax.psum_scatter(grad, "mp", scatter_dimension=0, tiled=True)
+
+    sums = in_vmem(sum_kernel, [shape16(96)], *kept(1, up4, down4, (mine,)), after=(grad,))
+    sums += in_vmem(
+        sum_kernel,
+        [jax.ShapeDtypeStruct((96, HALF), F32)], *kept(0, up5, down5, (sums[0],)),
+    )
+    wsum = sums[1] + send(sums[0], PARTNER).astype(F32)
     other = send(wsum[ROWS:], SIBLING)
     wgrad = jnp.where(
         core == 0,
@@ -372,17 +424,6 @@
     )
     new_logits, new_one, new_two = adam(wgrad, weight, probs, logits, moment_one, moment_two)
 
-    near = [start_of(dz, db) for dz in range(2) for db in (0, 1, 3)]
-    opposite = [(start_of(dz, 2), start_of(dz, 2) + 192) for dz in range(2)]
-    result, g0, g1, g3, g2, g4 = products(
-        acts, cot, None, near[:3] + list(opposite[0]), [384] * 3 + [192] * 2,
-        [line0, near0, far0, low0, high0],
-    )
-    result, h0, h1, h3 = products(
-        acts, cot, result, near[3:], [384] * 3, [line1, near1, far1]
-    )
-    result, h2, h4 = products(acts, cot, result, opposite[1], [192] * 2, [low1, high1])
-    grads = [g0, g1, g2, g4, g3, h0, h1, h2, h4, h3]
     result = result.astype(BF16)
     other = send(result[128:], SIBLING)
     output = jnp.where(
@@ -391,15 +432,6 @@
         jnp.concatenate([other, result[:128]], axis=1),
     )
 
-    mine, theirs = part(lies_at, grads)
-    grad = mine + send(theirs, SIBLING)
-
-    def quarter(r):
-        return lax.dynamic_slice_in_dim(grad, ((mp + r) % 4) * 768, 768, axis=0)
-
-    total = quarter(0)
-    for r in (1, 2, 3):
-        total = total + send(quarter(r), around(r))
     input_grad = total.astype(BF16).T
     return (output, input_grad, new_logits, new_one, new_two)
 

time: 212 us -> 195 us (0.920)
  waiting for transfers between devices: 105 us -> 78.9 us
  between operations: 1.21 us -> 14.4 us
  starting transfers between devices: 63.3 us -> 54.4 us
  Pallas kernels: 24.4 us -> 30.1 us
  local copies, waits for them, and re-layouts: 14.1 us -> 11.8 us
    ppermute x36 -> x34, waiting for transfers between devices: 105 us -> 78.9 us  [send(): return lax.ppermute(value, AXES, pairs)]
    ppermute x36 -> x34, starting transfers between devices: 63.3 us -> 54.4 us  [send(): return lax.ppermute(value, AXES, pairs)]
    pallas_call x10 -> x12, Pallas kernels: 18.5 us -> 24.2 us  [in_vmem(): pl.pallas_call(kernel, in_specs=[IN_VMEM] * len(args), out_specs=[IN_VMEM...]
    unnamed x68 -> x54, local copies, waits for them, and re-layouts: 12.3 us -> 10.1 us
  transfers between devices with their start and end apart: 36 -> 35, of which waited for: 13 -> 18; matrix products, arithmetic and copies ran while one was open for 3% -> 3% of each run, Pallas kernels for 8% -> 12%
where the time goes in v1:
time: 195 us
  waiting for transfers between devices  78.9 us (40%)
  starting transfers between devices  54.4 us (28%)
  Pallas kernels  30.1 us (15%)
  between operations  14.4 us (7%)
  local copies, waits for them, and re-layouts  11.8 us (6%)
  other arithmetic  5.05 us (3%)
    ppermute x34, waiting for transfers between devices, send(): return lax.ppermute(value, AXES, pairs)  78.9 us
    ppermute x34, starting transfers between devices, send(): return lax.ppermute(value, AXES, pairs)  54.4 us
    pallas_call x12, Pallas kernels, in_vmem(): pl.pallas_call(kernel, in_specs=[IN_VMEM] * len(args), out_specs=[IN_VMEM...  24.2 us
    unnamed x54, local copies, waits for them, and re-layouts  10.1 us
  transfers between devices with their start and end apart: 35, of which 18 were waited for; matrix products, arithmetic and copies ran while one was open for 3% of the time, Pallas kernels for 12%

profile of v1, /device:TPU:1, one launch (start us, length us, event | category | flops | bytes accessed | tf_op | source)
XLA Modules:
  0.0 194.7 jit_solution(17077963903528984102)
XLA Ops:
  7.2 1.3 copy-done.5
  12.5 3.3 %collective-permute-start.4 = (bf16[48,1536]{1,0:T(8,128)(2,1)S(1)}, bf16[48,1536]{1,0:T(8,128)(2,1)S(1)}, u32[]{:S(2)}, u32[]{:S(2)}) collective-permute-start(bf16[48,1536]{1,0:T(8,128)(2,1)S(1)} %get-tuple-element.92), channel_id=1, source_target_pairs={{0,4},{1,5},{2,6},{3,7},{4,0},{5,1},{6,2},{7,3},{8,12},{9,13},{10,... | collective-permute-start | bytes 442376 | tf_op jit(solution)/shard_map/ppermute | solution.py:69
  16.9 5.3 %collective-permute-start.8 = (bf16[96,1536]{1,0:T(8,128)(2,1)S(1)}, bf16[96,1536]{1,0:T(8,128)(2,1)S(1)}, u32[]{:S(2)}, u32[]{:S(2)}) collective-permute-start(bf16[96,1536]{1,0:T(8,128)(2,1)S(1)} %pad_maximum_fusion.3.refs_0_), channel_id=1, source_target_pairs={{0,128},{1,129},{2,130},{3,131},{4,132},{5,133},{6,134},{7,135},{8... | collective-permute-start | bytes 884744 | tf_op jit(solution)/shard_map/ppermute | solution.py:69
  22.7 1.6 collective-permute-start.1
  24.3 1.3 collective-permute-start.7
  25.6 2.6 %collective-permute-start.6 = (bf16[96,1536]{1,0:T(8,128)(2,1)S(1)}, bf16[96,1536]{1,0:T(8,128)(2,1)S(1)}, u32[]{:S(2)}, u32[]{:S(2)}) collective-permute-start(bf16[96,1536]{1,0:T(8,128)(2,1)S(1)} %pad_maximum_fusion.3.refs_0_), channel_id=1, source_target_pairs={{0,64},{1,65},{2,66},{3,67},{4,20},{5,21},{6,22},{7,23},{8,72},{9,... | collective-permute-start | bytes 884744 | tf_op jit(solution)/shard_map/ppermute | solution.py:69
  29.3 7.7 %collective-permute-done.8.refs_4_.refs_0_ = bf16[96,1536]{1,0:T(8,128)(2,1)S(1)} collective-permute-done((bf16[96,1536]{1,0:T(8,128)(2,1)S(1)}, bf16[96,1536]{1,0:T(8,128)(2,1)S(1)}, u32[]{:S(2)}, u32[]{:S(2)}) %collective-permute-start.8) | collective-permute-done | bytes 294944 | tf_op jit(solution)/shard_map/ppermute | solution.py:69
  37.0 1.3 collective-permute-start.13
  39.1 4.3 %collective-permute-start.3 = (bf16[128,1536]{1,0:T(8,128)(2,1)S(1)}, bf16[128,1536]{1,0:T(8,128)(2,1)}, u32[]{:S(2)}, u32[]{:S(2)}) collective-permute-start(bf16[128,1536]{1,0:T(8,128)(2,1)S(1)} %get-tuple-element.88), channel_id=1, source_target_pairs={{0,4},{1,5},{2,6},{3,7},{4,0},{5,1},{6,2},{7,3},{8,12},{9,13},{10,... | collective-permute-start | bytes 1179656 | tf_op jit(solution)/shard_map/ppermute | solution.py:69
  43.4 1.1 shard_map.220.refs_0_
  44.5 1.2 collective-permute-start.10
  45.7 1.5 collective-permute-start.9
  47.1 7.5 %collective-permute-done.1 = bf16[1536,128]{1,0:T(8,128)(2,1)S(1)} collective-permute-done((bf16[1536,128]{1,0:T(8,128)(2,1)S(1)}, bf16[1536,128]{1,0:T(8,128)(2,1)S(1)}, u32[]{:S(2)}, u32[]{:S(2)}) %collective-permute-start.1) | collective-permute-done | bytes 393248 | tf_op jit(solution)/shard_map/ppermute | solution.py:69
  54.6 2.8 %collective-permute-start.12 = (bf16[96,1536]{1,0:T(8,128)(2,1)S(1)}, bf16[96,1536]{1,0:T(8,128)(2,1)S(1)}, u32[]{:S(2)}, u32[]{:S(2)}) collective-permute-start(bf16[96,1536]{1,0:T(8,128)(2,1)S(1)} %collective-permute-done.8.refs_4_.refs_0_), channel_id=1, source_target_pairs={{0,64},{1,65},{2,66},{3,67},{4,20},{5,21},{6,22},{7,23},{8,72},{9,... | collective-permute-start | bytes 884744 | tf_op jit(solution)/shard_map/ppermute | solution.py:69
  58.3 6.9 %collective-permute-done.12.refs_2_ = bf16[96,1536]{1,0:T(8,128)(2,1)S(1)} collective-permute-done((bf16[96,1536]{1,0:T(8,128)(2,1)S(1)}, bf16[96,1536]{1,0:T(8,128)(2,1)S(1)}, u32[]{:S(2)}, u32[]{:S(2)}) %collective-permute-start.12) | collective-permute-done | bytes 294944 | tf_op jit(solution)/shard_map/ppermute | solution.py:69
  65.2 2.9 %collective-permute-done.11.refs_1_ = bf16[96,1536]{1,0:T(8,128)(2,1)S(1)} collective-permute-done((bf16[96,1536]{1,0:T(8,128)(2,1)S(1)}, bf16[96,1536]{1,0:T(8,128)(2,1)S(1)}, u32[]{:S(2)}, u32[]{:S(2)}) %collective-permute-start.11) | collective-permute-done | bytes 294944 | tf_op jit(solution)/shard_map/ppermute | solution.py:69
  68.2 1.3 collective-permute-start.17
  69.5 1.5 collective-permute-start.16
  72.6 1.2 pad_maximum_fusion.1.refs_1_.cot
  74.8 1.1 copy-done.16
  76.8 2.2 %shard_map.222 = (bf16[384,1536]{1,0:T(8,128)(2,1)S(1)}, bf16[384,1536]{1,0:T(8,128)(2,1)S(1)}) custom-call(bf16[3072,256]{1,0:T(8,128)(2,1)S(1)} %shard_map.218.refs_0_.acts, bf16[256,1536]{1,0:T(8,128)(2,1)S(1)} %pad_maximum_fusion.1.refs_1_.cot, bf16[384,1536]{1,0:T(8,128)(2,1)} %collective-permute-done.9.refs_2_.refs_1_, ...), custom_call_target="tpu_custom_call" | custom-call | bytes 1 | tf_op jit(solution)/shard_map/pallas_call | solution.py:272
  78.9 2.7 %collective-permute-start.14 = (bf16[384,1536]{1,0:T(8,128)(2,1)S(1)}, bf16[384,1536]{1,0:T(8,128)(2,1)S(1)}, u32[]{:S(2)}, u32[]{:S(2)}) collective-permute-start(bf16[384,1536]{1,0:T(8,128)(2,1)S(1)} %get-tuple-element.41), channel_id=1, source_target_pairs={{0,24},{1,25},{2,26},{3,27},{4,100},{5,101},{6,102},{7,103},{8,0},... | collective-permute-start | bytes 3538952 | tf_op jit(solution)/shard_map/ppermute | solution.py:69
  81.7 3.3 %collective-permute-done.17.refs_3_ = bf16[384,1536]{1,0:T(8,128)(2,1)} collective-permute-done((bf16[384,1536]{1,0:T(8,128)(2,1)S(1)}, bf16[384,1536]{1,0:T(8,128)(2,1)}, u32[]{:S(2)}, u32[]{:S(2)}) %collective-permute-start.17) | collective-permute-done | bytes 1179680 | tf_op jit(solution)/shard_map/ppermute | solution.py:69
  84.9 2.2 %shard_map.224 = (bf16[384,1536]{1,0:T(8,128)(2,1)S(1)}, bf16[384,1536]{1,0:T(8,128)(2,1)S(1)}) custom-call(bf16[3072,256]{1,0:T(8,128)(2,1)S(1)} %shard_map.218.refs_0_.acts, bf16[256,1536]{1,0:T(8,128)(2,1)S(1)} %pad_maximum_fusion.1.refs_1_.cot, bf16[384,1536]{1,0:T(8,128)(2,1)} %collective-permute-done.16.refs_2_, ...), custom_call_target="tpu_custom_call" | custom-call | bytes 1 | tf_op jit(solution)/shard_map/pallas_call | solution.py:272
  87.1 2.8 %collective-permute-start.18 = (bf16[384,1536]{1,0:T(8,128)(2,1)S(1)}, bf16[384,1536]{1,0:T(8,128)(2,1)S(1)}, u32[]{:S(2)}, u32[]{:S(2)}) collective-permute-start(bf16[384,1536]{1,0:T(8,128)(2,1)S(1)} %get-tuple-element.44), channel_id=1, source_target_pairs={{0,24},{1,25},{2,26},{3,27},{4,100},{5,101},{6,102},{7,103},{8,0},... | collective-permute-start | bytes 3538952 | tf_op jit(solution)/shard_map/ppermute | solution.py:69
  89.9 7.6 %collective-permute-done.14.refs_3_ = bf16[384,1536]{1,0:T(8,128)(2,1)S(1)} collective-permute-done((bf16[384,1536]{1,0:T(8,128)(2,1)S(1)}, bf16[384,1536]{1,0:T(8,128)(2,1)S(1)}, u32[]{:S(2)}, u32[]{:S(2)}) %collective-permute-start.14) | collective-permute-done | bytes 1179680 | tf_op jit(solution)/shard_map/ppermute | solution.py:69
  98.2 5.1 %shard_map.223 = (f32[256,1536]{1,0:T(8,128)S(1)}, f32[384,256]{1,0:T(8,128)S(1)}, f32[384,256]{1,0:T(8,128)S(1)}, f32[384,256]{1,0:T(8,128)S(1)}, f32[192,256]{1,0:T(8,128)S(1)}, /*index=5*/f32[192,256]{1,0:T(8,128)S(1)}) custom-call(bf16[3072,256]{1,0:T(8,128)(2,1)S(1)} %shard_map.218.refs_0_.acts, bf16[256,1536]{1,0:T(8,128)(2,1)S(1)} %pad_maximum_fusion.1.refs_1_.cot, ...), custom_call_target="tpu_custom_call" | custom-call | bytes 1 | tf_op jit(solution)/shard_map/pallas_call | solution.py:272
  103.4 6.7 %collective-permute-done.18.refs_4_.refs_3_ = bf16[384,1536]{1,0:T(8,128)(2,1)S(1)} collective-permute-done((bf16[384,1536]{1,0:T(8,128)(2,1)S(1)}, bf16[384,1536]{1,0:T(8,128)(2,1)S(1)}, u32[]{:S(2)}, u32[]{:S(2)}) %collective-permute-start.18) | collective-permute-done | bytes 1179680 | tf_op jit(solution)/shard_map/ppermute | solution.py:69
  110.9 4.8 %shard_map.225 = (f32[256,1536]{1,0:T(8,128)S(1)}, f32[384,256]{1,0:T(8,128)S(1)}, f32[384,256]{1,0:T(8,128)S(1)}, f32[384,256]{1,0:T(8,128)S(1)}, f32[192,256]{1,0:T(8,128)S(1)}, /*index=5*/f32[192,256]{1,0:T(8,128)S(1)}) custom-call(bf16[3072,256]{1,0:T(8,128)(2,1)S(1)} %shard_map.218.refs_0_.acts, bf16[256,1536]{1,0:T(8,128)(2,1)S(1)} %pad_maximum_fusion.1.refs_1_.cot, ...), custom_call_target="tpu_custom_call" | custom-call | bytes 1 | tf_op jit(solution)/shard_map/pallas_call | solution.py:272
  116.8 1.1 collective-permute-start.21
  118.0 2.1 %shard_map.228 = (bf16[384,1536]{1,0:T(8,128)(2,1)}, bf16[384,1536]{1,0:T(8,128)(2,1)}) custom-call(bf16[3072,256]{1,0:T(8,128)(2,1)S(1)} %shard_map.218.refs_0_.acts, bf16[256,1536]{1,0:T(8,128)(2,1)S(1)} %pad_maximum_fusion.1.refs_1_.cot, bf16[384,1536]{1,0:T(8,128)(2,1)S(1)} %collective-permute-done.15.refs_4_.refs_2_, ...), custom_call_target="tpu_custom_call" | custom-call | bytes 1 | tf_op jit(solution)/shard_map/pallas_call | solution.py:272
  120.1 2.6 %collective-permute-start.25 = (bf16[384,1536]{1,0:T(8,128)(2,1)}, bf16[384,1536]{1,0:T(8,128)(2,1)}, u32[]{:S(2)}, u32[]{:S(2)}) collective-permute-start(bf16[384,1536]{1,0:T(8,128)(2,1)} %get-tuple-element.62), channel_id=1, source_target_pairs={{0,24},{1,25},{2,26},{3,27},{4,100},{5,101},{6,102},{7,103},{8,0},... | collective-permute-start | bytes 3538952 | tf_op jit(solution)/shard_map/ppermute | solution.py:69
  122.7 2.1 %shard_map.227 = (bf16[384,1536]{1,0:T(8,128)(2,1)}, bf16[384,1536]{1,0:T(8,128)(2,1)}) custom-call(bf16[3072,256]{1,0:T(8,128)(2,1)S(1)} %shard_map.218.refs_0_.acts, bf16[256,1536]{1,0:T(8,128)(2,1)S(1)} %pad_maximum_fusion.1.refs_1_.cot, bf16[384,1536]{1,0:T(8,128)(2,1)S(1)} %collective-permute-done.19.refs_5_.refs_2_, ...), custom_call_target="tpu_custom_call" | custom-call | bytes 1 | tf_op jit(solution)/shard_map/pallas_call | solution.py:272
  124.8 2.7 %collective-permute-start.23 = (bf16[384,1536]{1,0:T(8,128)(2,1)}, bf16[384,1536]{1,0:T(8,128)(2,1)}, u32[]{:S(2)}, u32[]{:S(2)}) collective-permute-start(bf16[384,1536]{1,0:T(8,128)(2,1)} %get-tuple-element.60), channel_id=1, source_target_pairs={{0,24},{1,25},{2,26},{3,27},{4,100},{5,101},{6,102},{7,103},{8,0},... | collective-permute-start | bytes 3538952 | tf_op jit(solution)/shard_map/ppermute | solution.py:69
  127.5 1.3 add.137.refs_4_
  128.9 8.1 %collective-permute-done.24.refs_2_ = bf16[384,1536]{1,0:T(8,128)(2,1)} collective-permute-done((bf16[384,1536]{1,0:T(8,128)(2,1)}, bf16[384,1536]{1,0:T(8,128)(2,1)}, u32[]{:S(2)}, u32[]{:S(2)}) %collective-permute-start.24) | collective-permute-done | bytes 1179680 | tf_op jit(solution)/shard_map/ppermute | solution.py:69
  136.9 1.4 copy-done.4
  138.4 2.4 %shard_map.229 = (f32[96,1536]{1,0:T(8,128)S(1)}, bf16[96,1536]{1,0:T(8,128)(2,1)S(1)}, bf16[96,1536]{1,0:T(8,128)(2,1)S(1)}, bf16[96,1536]{1,0:T(8,128)(2,1)S(1)}) custom-call(bf16[3072,256]{1,0:T(8,128)(2,1)S(1)} %shard_map.218.refs_0_.acts, bf16[256,1536]{1,0:T(8,128)(2,1)S(1)} %pad_maximum_fusion.1.refs_1_.cot, ...), custom_call_target="tpu_custom_call" | custom-call | bytes 1 | tf_op jit(solution)/shard_map/pallas_call | solution.py:272
  141.1 2.8 %collective-permute-start.27 = (bf16[96,1536]{1,0:T(8,128)(2,1)S(1)}, bf16[96,1536]{1,0:T(8,128)(2,1)S(1)}, u32[]{:S(2)}, u32[]{:S(2)}) collective-permute-start(bf16[96,1536]{1,0:T(8,128)(2,1)S(1)} %get-tuple-element.65), channel_id=1, source_target_pairs={{0,64},{1,65},{2,66},{3,67},{4,20},{5,21},{6,22},{7,23},{8,72},{9,... | collective-permute-start | bytes 884744 | tf_op jit(solution)/shard_map/ppermute | solution.py:69
  144.6 6.7 %collective-permute-done.26.refs_1_ = bf16[96,1536]{1,0:T(8,128)(2,1)S(1)} collective-permute-done((bf16[96,1536]{1,0:T(8,128)(2,1)S(1)}, bf16[96,1536]{1,0:T(8,128)(2,1)S(1)}, u32[]{:S(2)}, u32[]{:S(2)}) %collective-permute-start.26) | collective-permute-done | bytes 294944 | tf_op jit(solution)/shard_map/ppermute | solution.py:69
  151.2 5.0 %collective-permute-done.27.refs_2_ = bf16[96,1536]{1,0:T(8,128)(2,1)S(1)} collective-permute-done((bf16[96,1536]{1,0:T(8,128)(2,1)S(1)}, bf16[96,1536]{1,0:T(8,128)(2,1)S(1)}, u32[]{:S(2)}, u32[]{:S(2)}) %collective-permute-start.27) | collective-permute-done | bytes 294944 | tf_op jit(solution)/shard_map/ppermute | solution.py:69
  156.4 2.7 %collective-permute-start.32 = (bf16[96,1536]{1,0:T(8,128)(2,1)S(1)}, bf16[96,1536]{1,0:T(8,128)(2,1)S(1)}, u32[]{:S(2)}, u32[]{:S(2)}) collective-permute-start(bf16[96,1536]{1,0:T(8,128)(2,1)S(1)} %shard_map.230.refs_4_), channel_id=1, source_target_pairs={{0,128},{1,129},{2,130},{3,131},{4,132},{5,133},{6,134},{7,135},{8... | collective-permute-start | bytes 884744 | tf_op jit(solution)/shard_map/ppermute | solution.py:69
  159.1 1.9 shard_map.231
  161.1 2.5 %collective-permute-start.30 = (bf16[96,1536]{1,0:T(8,128)(2,1)S(1)}, bf16[96,1536]{1,0:T(8,128)(2,1)S(1)}, u32[]{:S(2)}, u32[]{:S(2)}) collective-permute-start(bf16[96,1536]{1,0:T(8,128)(2,1)S(1)} %get-tuple-element.69), channel_id=1, source_target_pairs={{0,64},{1,65},{2,66},{3,67},{4,20},{5,21},{6,22},{7,23},{8,72},{9,... | collective-permute-start | bytes 884744 | tf_op jit(solution)/shard_map/ppermute | solution.py:69
  163.6 1.7 collective-permute-start.31
  165.9 5.5 %collective-permute-done.29.one = bf16[96,1536]{1,0:T(8,128)(2,1)S(1)} collective-permute-done((bf16[96,1536]{1,0:T(8,128)(2,1)S(1)}, bf16[96,1536]{1,0:T(8,128)(2,1)S(1)}, u32[]{:S(2)}, u32[]{:S(2)}) %collective-permute-start.29) | collective-permute-done | bytes 294944 | tf_op jit(solution)/shard_map/ppermute | solution.py:69
  172.1 7.6 %collective-permute-done.32 = bf16[96,1536]{1,0:T(8,128)(2,1)S(1)} collective-permute-done((bf16[96,1536]{1,0:T(8,128)(2,1)S(1)}, bf16[96,1536]{1,0:T(8,128)(2,1)S(1)}, u32[]{:S(2)}, u32[]{:S(2)}) %collective-permute-start.32) | collective-permute-done | bytes 294944 | tf_op jit(solution)/shard_map/ppermute | solution.py:69
  182.6 3.4 %shard_map.233 = (f32[6,12,3072]{2,1,0:T(8,128)}, f32[6,12,3072]{2,1,0:T(8,128)}, f32[6,12,3072]{2,1,0:T(8,128)}) custom-call(f32[48,3072]{1,0:T(8,128)S(1)} %maximum_select_fusion.1.wgrad, bf16[48,3072]{1,0:T(8,128)(2,1)S(1)} %copy-done.10, f32[6,12,3072]{2,1,0:T(8,128)S(1)} %copy-done.14, f32[6,12,3072]{2,1,0:T(8,128)S(1)} %copy-done.6, ...), custom_call_target="tpu_custom_call" | custom-call | bytes 1 | tf_op jit(solution)/shard_map/pallas_call | solution.py:155
  (113 shorter events, 21.8 us)
Async XLA Ops:
  7.2 178.8 %reduce-scatter.2.cloned.1.call-start = ((), (), s32[]{:S(2)}) async-start(), calls=%async_computation.1 | async-start | bytes 1966080 | tf_op jit(solution)/shard_map/reduce_scatter | solution.py:411
  10.5 5.3 %copy-start.19 = (bf16[128,768]{1,0:T(8,128)(2,1)S(1)}, bf16[128,768]{1,0:T(8,128)(2,1)}, u32[]{:S(2)}) copy-start(bf16[128,768]{1,0:T(8,128)(2,1)} %param.19) | copy-start | bytes 589828
  12.5 25.8 %copy-start.18 = (bf16[128,3072]{1,0:T(8,128)(2,1)S(1)}, bf16[128,3072]{1,0:T(8,128)(2,1)}, u32[]{:S(2)}) copy-start(bf16[128,3072]{1,0:T(8,128)(2,1)} %param.23) | copy-start | bytes 2359300
  12.5 4.3 %collective-permute-start.4 = (bf16[48,1536]{1,0:T(8,128)(2,1)S(1)}, bf16[48,1536]{1,0:T(8,128)(2,1)S(1)}, u32[]{:S(2)}, u32[]{:S(2)}) collective-permute-start(bf16[48,1536]{1,0:T(8,128)(2,1)S(1)} %get-tuple-element.92), channel_id=1, source_target_pairs={{0,4},{1,5},{2,6},{3,7},{4,0},{5,1},{6,2},{7,3},{8,12},{9,13},{10,... | collective-permute-start | bytes 442376 | tf_op jit(solution)/shard_map/ppermute | solution.py:69
  16.0 6.6 %collective-permute-start = (bf16[768,128]{1,0:T(8,128)(2,1)S(1)}, bf16[768,128]{1,0:T(8,128)(2,1)S(1)}, u32[]{:S(2)}, u32[]{:S(2)}) collective-permute-start(bf16[768,128]{1,0:T(8,128)(2,1)S(1)} %bitcast.13), channel_id=1, source_target_pairs={{0,1},{1,0},{2,3},{3,2},{4,5},{5,4},{6,7},{7,6},{8,9},{9,8},{10,11... | collective-permute-start | bytes 589832 | tf_op jit(solution)/shard_map/ppermute | solution.py:69
  16.9 20.1 %collective-permute-start.8 = (bf16[96,1536]{1,0:T(8,128)(2,1)S(1)}, bf16[96,1536]{1,0:T(8,128)(2,1)S(1)}, u32[]{:S(2)}, u32[]{:S(2)}) collective-permute-start(bf16[96,1536]{1,0:T(8,128)(2,1)S(1)} %pad_maximum_fusion.3.refs_0_), channel_id=1, source_target_pairs={{0,128},{1,129},{2,130},{3,131},{4,132},{5,133},{6,134},{7,135},{8... | collective-permute-start | bytes 884744 | tf_op jit(solution)/shard_map/ppermute | solution.py:69
  22.7 31.9 %collective-permute-start.1 = (bf16[1536,128]{1,0:T(8,128)(2,1)S(1)}, bf16[1536,128]{1,0:T(8,128)(2,1)S(1)}, u32[]{:S(2)}, u32[]{:S(2)}) collective-permute-start(bf16[1536,128]{1,0:T(8,128)(2,1)S(1)} %pad_maximum_fusion.2.refs_5_), channel_id=1, source_target_pairs={{0,2},{1,3},{2,0},{3,1},{4,6},{5,7},{6,4},{7,5},{8,10},{9,11},{10,... | collective-permute-start | bytes 1179656 | tf_op jit(solution)/shard_map/ppermute | solution.py:69
  24.3 14.8 %collective-permute-start.7 = (bf16[96,1536]{1,0:T(8,128)(2,1)S(1)}, bf16[96,1536]{1,0:T(8,128)(2,1)S(1)}, u32[]{:S(2)}, u32[]{:S(2)}) collective-permute-start(bf16[96,1536]{1,0:T(8,128)(2,1)S(1)} %pad_maximum_fusion.3.refs_0_), channel_id=1, source_target_pairs={{0,32},{1,33},{2,34},{3,35},{4,12},{5,13},{6,14},{7,15},{8,40},{9,... | collective-permute-start | bytes 884744 | tf_op jit(solution)/shard_map/ppermute | solution.py:69
  25.6 17.8 %collective-permute-start.6 = (bf16[96,1536]{1,0:T(8,128)(2,1)S(1)}, bf16[96,1536]{1,0:T(8,128)(2,1)S(1)}, u32[]{:S(2)}, u32[]{:S(2)}) collective-permute-start(bf16[96,1536]{1,0:T(8,128)(2,1)S(1)} %pad_maximum_fusion.3.refs_0_), channel_id=1, source_target_pairs={{0,64},{1,65},{2,66},{3,67},{4,20},{5,21},{6,22},{7,23},{8,72},{9,... | collective-permute-start | bytes 884744 | tf_op jit(solution)/shard_map/ppermute | solution.py:69
  28.2 15.2 %collective-permute-start.5 = (bf16[96,1536]{1,0:T(8,128)(2,1)S(1)}, bf16[96,1536]{1,0:T(8,128)(2,1)S(1)}, u32[]{:S(2)}, u32[]{:S(2)}) collective-permute-start(bf16[96,1536]{1,0:T(8,128)(2,1)S(1)} %pad_maximum_fusion.3.refs_0_), channel_id=1, source_target_pairs={{0,96},{1,97},{2,98},{3,99},{4,28},{5,29},{6,30},{7,31},{8,104},{9... | collective-permute-start | bytes 884744 | tf_op jit(solution)/shard_map/ppermute | solution.py:69
  37.0 20.4 %collective-permute-start.13 = (bf16[96,1536]{1,0:T(8,128)(2,1)S(1)}, bf16[96,1536]{1,0:T(8,128)(2,1)S(1)}, u32[]{:S(2)}, u32[]{:S(2)}) collective-permute-start(bf16[96,1536]{1,0:T(8,128)(2,1)S(1)} %collective-permute-done.8.refs_4_.refs_0_), channel_id=1, source_target_pairs={{0,32},{1,33},{2,34},{3,35},{4,12},{5,13},{6,14},{7,15},{8,40},{9,... | collective-permute-start | bytes 884744 | tf_op jit(solution)/shard_map/ppermute | solution.py:69
  39.1 31.9 %collective-permute-start.3 = (bf16[128,1536]{1,0:T(8,128)(2,1)S(1)}, bf16[128,1536]{1,0:T(8,128)(2,1)}, u32[]{:S(2)}, u32[]{:S(2)}) collective-permute-start(bf16[128,1536]{1,0:T(8,128)(2,1)S(1)} %get-tuple-element.88), channel_id=1, source_target_pairs={{0,4},{1,5},{2,6},{3,7},{4,0},{5,1},{6,2},{7,3},{8,12},{9,13},{10,... | collective-permute-start | bytes 1179656 | tf_op jit(solution)/shard_map/ppermute | solution.py:69
  44.5 32.3 %collective-permute-start.10 = (bf16[384,1536]{1,0:T(8,128)(2,1)}, bf16[384,1536]{1,0:T(8,128)(2,1)}, u32[]{:S(2)}, u32[]{:S(2)}) collective-permute-start(bf16[384,1536]{1,0:T(8,128)(2,1)} %shard_map.220.refs_0_), channel_id=1, source_target_pairs={{0,8},{1,9},{2,10},{3,11},{4,36},{5,37},{6,38},{7,39},{8,16},{9,17... | collective-permute-start | bytes 3538952 | tf_op jit(solution)/shard_map/ppermute | solution.py:69
  45.7 31.1 %collective-permute-start.9 = (bf16[384,1536]{1,0:T(8,128)(2,1)}, bf16[384,1536]{1,0:T(8,128)(2,1)}, u32[]{:S(2)}, u32[]{:S(2)}) collective-permute-start(bf16[384,1536]{1,0:T(8,128)(2,1)} %shard_map.220.refs_0_), channel_id=1, source_target_pairs={{0,24},{1,25},{2,26},{3,27},{4,100},{5,101},{6,102},{7,103},{8,0},... | collective-permute-start | bytes 3538952 | tf_op jit(solution)/shard_map/ppermute | solution.py:69
  54.6 10.6 %collective-permute-start.12 = (bf16[96,1536]{1,0:T(8,128)(2,1)S(1)}, bf16[96,1536]{1,0:T(8,128)(2,1)S(1)}, u32[]{:S(2)}, u32[]{:S(2)}) collective-permute-start(bf16[96,1536]{1,0:T(8,128)(2,1)S(1)} %collective-permute-done.8.refs_4_.refs_0_), channel_id=1, source_target_pairs={{0,64},{1,65},{2,66},{3,67},{4,20},{5,21},{6,22},{7,23},{8,72},{9,... | collective-permute-start | bytes 884744 | tf_op jit(solution)/shard_map/ppermute | solution.py:69
  57.4 10.7 %collective-permute-start.11 = (bf16[96,1536]{1,0:T(8,128)(2,1)S(1)}, bf16[96,1536]{1,0:T(8,128)(2,1)S(1)}, u32[]{:S(2)}, u32[]{:S(2)}) collective-permute-start(bf16[96,1536]{1,0:T(8,128)(2,1)S(1)} %collective-permute-done.8.refs_4_.refs_0_), channel_id=1, source_target_pairs={{0,96},{1,97},{2,98},{3,99},{4,28},{5,29},{6,30},{7,31},{8,104},{9... | collective-permute-start | bytes 884744 | tf_op jit(solution)/shard_map/ppermute | solution.py:69
  58.2 12.7 %copy-start.1 = (bf16[3072,128]{1,0:T(8,128)(2,1)}, bf16[3072,128]{1,0:T(8,128)(2,1)S(1)}, u32[]{:S(2)}) copy-start(bf16[3072,128]{1,0:T(8,128)(2,1)S(1)} %pad_maximum_fusion.mine.refs_4_) | copy-start | bytes 2359300
  58.3 13.5 %copy-start.20 = (s32[64]{0:T(128)S(1)}, s32[64]{0:T(128)}, u32[]{:S(2)}) copy-start(s32[64]{0:T(128)} %constant.124.clone) | copy-start | bytes 772
  58.3 13.5 %copy-start.21 = (s32[64]{0:T(128)S(1)}, s32[64]{0:T(128)}, u32[]{:S(2)}) copy-start(s32[64]{0:T(128)} %constant.123.clone) | copy-start | bytes 772
  58.3 13.5 %copy-start.22 = (s32[64]{0:T(128)S(1)}, s32[64]{0:T(128)}, u32[]{:S(2)}) copy-start(s32[64]{0:T(128)} %constant.122.clone) | copy-start | bytes 772
  58.3 13.5 %copy-start.23 = (s32[64]{0:T(128)S(1)}, s32[64]{0:T(128)}, u32[]{:S(2)}) copy-start(s32[64]{0:T(128)} %constant.121.clone) | copy-start | bytes 772
  58.3 13.5 %copy-start.24 = (s32[64]{0:T(128)S(1)}, s32[64]{0:T(128)}, u32[]{:S(2)}) copy-start(s32[64]{0:T(128)} %constant.120.clone) | copy-start | bytes 772
  58.3 13.5 %copy-start.25 = (s32[64]{0:T(128)S(1)}, s32[64]{0:T(128)}, u32[]{:S(2)}) copy-start(s32[64]{0:T(128)} %constant.119.clone) | copy-start | bytes 772
  68.2 16.7 %collective-permute-start.17 = (bf16[384,1536]{1,0:T(8,128)(2,1)S(1)}, bf16[384,1536]{1,0:T(8,128)(2,1)}, u32[]{:S(2)}, u32[]{:S(2)}) collective-permute-start(bf16[384,1536]{1,0:T(8,128)(2,1)S(1)} %shard_map.221.refs_4_.refs_1_), channel_id=1, source_target_pairs={{0,8},{1,9},{2,10},{3,11},{4,36},{5,37},{6,38},{7,39},{8,16},{9,17... | collective-permute-start | bytes 3538952 | tf_op jit(solution)/shard_map/ppermute | solution.py:69
  69.5 15.5 %collective-permute-start.16 = (bf16[384,1536]{1,0:T(8,128)(2,1)S(1)}, bf16[384,1536]{1,0:T(8,128)(2,1)}, u32[]{:S(2)}, u32[]{:S(2)}) collective-permute-start(bf16[384,1536]{1,0:T(8,128)(2,1)S(1)} %shard_map.221.refs_4_.refs_1_), channel_id=1, source_target_pairs={{0,24},{1,25},{2,26},{3,27},{4,100},{5,101},{6,102},{7,103},{8,0},... | collective-permute-start | bytes 3538952 | tf_op jit(solution)/shard_map/ppermute | solution.py:69
  70.9 2.9 %collective-permute-start.2 = (bf16[3072,128]{1,0:T(8,128)(2,1)S(1)}, bf16[3072,128]{1,0:T(8,128)(2,1)S(1)}, u32[]{:S(2)}, u32[]{:S(2)}) collective-permute-start(bf16[3072,128]{1,0:T(8,128)(2,1)S(1)} %pad_maximum_fusion.mine.refs_4_), channel_id=1, source_target_pairs={{0,4},{1,5},{2,6},{3,7},{4,0},{5,1},{6,2},{7,3},{8,12},{9,13},{10,... | collective-permute-start | bytes 2359304 | tf_op jit(solution)/shard_map/ppermute | solution.py:69
  78.9 18.5 %collective-permute-start.14 = (bf16[384,1536]{1,0:T(8,128)(2,1)S(1)}, bf16[384,1536]{1,0:T(8,128)(2,1)S(1)}, u32[]{:S(2)}, u32[]{:S(2)}) collective-permute-start(bf16[384,1536]{1,0:T(8,128)(2,1)S(1)} %get-tuple-element.41), channel_id=1, source_target_pairs={{0,24},{1,25},{2,26},{3,27},{4,100},{5,101},{6,102},{7,103},{8,0},... | collective-permute-start | bytes 3538952 | tf_op jit(solution)/shard_map/ppermute | solution.py:69
  81.7 16.6 %collective-permute-start.15 = (bf16[384,1536]{1,0:T(8,128)(2,1)S(1)}, bf16[384,1536]{1,0:T(8,128)(2,1)S(1)}, u32[]{:S(2)}, u32[]{:S(2)}) collective-permute-start(bf16[384,1536]{1,0:T(8,128)(2,1)S(1)} %get-tuple-element.42.refs_4_), channel_id=1, source_target_pairs={{0,8},{1,9},{2,10},{3,11},{4,36},{5,37},{6,38},{7,39},{8,16},{9,17... | collective-permute-start | bytes 3538952 | tf_op jit(solution)/shard_map/ppermute | solution.py:69
  87.1 23.0 %collective-permute-start.18 = (bf16[384,1536]{1,0:T(8,128)(2,1)S(1)}, bf16[384,1536]{1,0:T(8,128)(2,1)S(1)}, u32[]{:S(2)}, u32[]{:S(2)}) collective-permute-start(bf16[384,1536]{1,0:T(8,128)(2,1)S(1)} %get-tuple-element.44), channel_id=1, source_target_pairs={{0,24},{1,25},{2,26},{3,27},{4,100},{5,101},{6,102},{7,103},{8,0},... | collective-permute-start | bytes 3538952 | tf_op jit(solution)/shard_map/ppermute | solution.py:69
  89.9 21.0 %collective-permute-start.19 = (bf16[384,1536]{1,0:T(8,128)(2,1)S(1)}, bf16[384,1536]{1,0:T(8,128)(2,1)S(1)}, u32[]{:S(2)}, u32[]{:S(2)}) collective-permute-start(bf16[384,1536]{1,0:T(8,128)(2,1)S(1)} %get-tuple-element.45.refs_4_), channel_id=1, source_target_pairs={{0,8},{1,9},{2,10},{3,11},{4,36},{5,37},{6,38},{7,39},{8,16},{9,17... | collective-permute-start | bytes 3538952 | tf_op jit(solution)/shard_map/ppermute | solution.py:69
  116.8 10.7 %copy-start.3 = (f32[3072,128]{1,0:T(8,128)}, f32[3072,128]{1,0:T(8,128)S(1)}, u32[]{:S(2)}) copy-start(f32[3072,128]{1,0:T(8,128)S(1)} %get-tuple-element.57.refs_4_) | copy-start | bytes 4718596
  116.8 10.7 %collective-permute-start.21 = (f32[3072,128]{1,0:T(8,128)S(1)}, f32[3072,128]{1,0:T(8,128)S(1)}, u32[]{:S(2)}, u32[]{:S(2)}) collective-permute-start(f32[3072,128]{1,0:T(8,128)S(1)} %get-tuple-element.58), channel_id=1, source_target_pairs={{0,4},{1,5},{2,6},{3,7},{4,0},{5,1},{6,2},{7,3},{8,12},{9,13},{10,... | collective-permute-start | bytes 4718600 | tf_op jit(solution)/shard_map/ppermute | solution.py:69
  120.1 16.9 %collective-permute-start.24 = (bf16[384,1536]{1,0:T(8,128)(2,1)}, bf16[384,1536]{1,0:T(8,128)(2,1)}, u32[]{:S(2)}, u32[]{:S(2)}) collective-permute-start(bf16[384,1536]{1,0:T(8,128)(2,1)} %get-tuple-element.61), channel_id=1, source_target_pairs={{0,8},{1,9},{2,10},{3,11},{4,36},{5,37},{6,38},{7,39},{8,16},{9,17... | collective-permute-start | bytes 3538952 | tf_op jit(solution)/shard_map/ppermute | solution.py:69
  120.1 16.8 %collective-permute-start.25 = (bf16[384,1536]{1,0:T(8,128)(2,1)}, bf16[384,1536]{1,0:T(8,128)(2,1)}, u32[]{:S(2)}, u32[]{:S(2)}) collective-permute-start(bf16[384,1536]{1,0:T(8,128)(2,1)} %get-tuple-element.62), channel_id=1, source_target_pairs={{0,24},{1,25},{2,26},{3,27},{4,100},{5,101},{6,102},{7,103},{8,0},... | collective-permute-start | bytes 3538952 | tf_op jit(solution)/shard_map/ppermute | solution.py:69
  124.8 34.3 %collective-permute-start.22 = (bf16[384,1536]{1,0:T(8,128)(2,1)}, bf16[384,1536]{1,0:T(8,128)(2,1)S(1)}, u32[]{:S(2)}, u32[]{:S(2)}) collective-permute-start(bf16[384,1536]{1,0:T(8,128)(2,1)} %get-tuple-element.59), channel_id=1, source_target_pairs={{0,8},{1,9},{2,10},{3,11},{4,36},{5,37},{6,38},{7,39},{8,16},{9,17... | collective-permute-start | bytes 3538952 | tf_op jit(solution)/shard_map/ppermute | solution.py:69
  124.8 34.3 %collective-permute-start.23 = (bf16[384,1536]{1,0:T(8,128)(2,1)}, bf16[384,1536]{1,0:T(8,128)(2,1)}, u32[]{:S(2)}, u32[]{:S(2)}) collective-permute-start(bf16[384,1536]{1,0:T(8,128)(2,1)} %get-tuple-element.60), channel_id=1, source_target_pairs={{0,24},{1,25},{2,26},{3,27},{4,100},{5,101},{6,102},{7,103},{8,0},... | collective-permute-start | bytes 3538952 | tf_op jit(solution)/shard_map/ppermute | solution.py:69
  138.4 6.1 %copy-start.8 = (f32[256,1536]{1,0:T(8,128)S(1)}, f32[256,1536]{1,0:T(8,128)}, u32[]{:S(2)}) copy-start(f32[256,1536]{1,0:T(8,128)} %copy-done.7) | copy-start | bytes 4718596
  140.7 10.5 %collective-permute-start.26 = (bf16[96,1536]{1,0:T(8,128)(2,1)S(1)}, bf16[96,1536]{1,0:T(8,128)(2,1)S(1)}, u32[]{:S(2)}, u32[]{:S(2)}) collective-permute-start(bf16[96,1536]{1,0:T(8,128)(2,1)S(1)} %get-tuple-element.64), channel_id=1, source_target_pairs={{0,32},{1,33},{2,34},{3,35},{4,12},{5,13},{6,14},{7,15},{8,40},{9,... | collective-permute-start | bytes 884744 | tf_op jit(solution)/shard_map/ppermute | solution.py:69
  141.1 15.2 %collective-permute-start.27 = (bf16[96,1536]{1,0:T(8,128)(2,1)S(1)}, bf16[96,1536]{1,0:T(8,128)(2,1)S(1)}, u32[]{:S(2)}, u32[]{:S(2)}) collective-permute-start(bf16[96,1536]{1,0:T(8,128)(2,1)S(1)} %get-tuple-element.65), channel_id=1, source_target_pairs={{0,64},{1,65},{2,66},{3,67},{4,20},{5,21},{6,22},{7,23},{8,72},{9,... | collective-permute-start | bytes 884744 | tf_op jit(solution)/shard_map/ppermute | solution.py:69
  143.8 12.5 %collective-permute-start.28 = (bf16[96,1536]{1,0:T(8,128)(2,1)S(1)}, bf16[96,1536]{1,0:T(8,128)(2,1)S(1)}, u32[]{:S(2)}, u32[]{:S(2)}) collective-permute-start(bf16[96,1536]{1,0:T(8,128)(2,1)S(1)} %get-tuple-element.66), channel_id=1, source_target_pairs={{0,96},{1,97},{2,98},{3,99},{4,28},{5,29},{6,30},{7,31},{8,104},{9... | collective-permute-start | bytes 884744 | tf_op jit(solution)/shard_map/ppermute | solution.py:69
  144.5 11.8 %copy-start = (f32[3072,128]{1,0:T(8,128)S(1)}, f32[3072,128]{1,0:T(8,128)}, u32[]{:S(2)}) copy-start(f32[3072,128]{1,0:T(8,128)} %add.137.refs_4_) | copy-start | bytes 4718596
  156.4 23.2 %collective-permute-start.32 = (bf16[96,1536]{1,0:T(8,128)(2,1)S(1)}, bf16[96,1536]{1,0:T(8,128)(2,1)S(1)}, u32[]{:S(2)}, u32[]{:S(2)}) collective-permute-start(bf16[96,1536]{1,0:T(8,128)(2,1)S(1)} %shard_map.230.refs_4_), channel_id=1, source_target_pairs={{0,128},{1,129},{2,130},{3,131},{4,132},{5,133},{6,134},{7,135},{8... | collective-permute-start | bytes 884744 | tf_op jit(solution)/shard_map/ppermute | solution.py:69
  161.0 10.3 %collective-permute-start.29 = (bf16[96,1536]{1,0:T(8,128)(2,1)S(1)}, bf16[96,1536]{1,0:T(8,128)(2,1)S(1)}, u32[]{:S(2)}, u32[]{:S(2)}) collective-permute-start(bf16[96,1536]{1,0:T(8,128)(2,1)S(1)} %get-tuple-element.68), channel_id=1, source_target_pairs={{0,32},{1,33},{2,34},{3,35},{4,12},{5,13},{6,14},{7,15},{8,40},{9,... | collective-permute-start | bytes 884744 | tf_op jit(solution)/shard_map/ppermute | solution.py:69
  161.1 10.2 %collective-permute-start.30 = (bf16[96,1536]{1,0:T(8,128)(2,1)S(1)}, bf16[96,1536]{1,0:T(8,128)(2,1)S(1)}, u32[]{:S(2)}, u32[]{:S(2)}) collective-permute-start(bf16[96,1536]{1,0:T(8,128)(2,1)S(1)} %get-tuple-element.69), channel_id=1, source_target_pairs={{0,64},{1,65},{2,66},{3,67},{4,20},{5,21},{6,22},{7,23},{8,72},{9,... | collective-permute-start | bytes 884744 | tf_op jit(solution)/shard_map/ppermute | solution.py:69
  163.6 8.4 %collective-permute-start.31 = (bf16[96,1536]{1,0:T(8,128)(2,1)S(1)}, bf16[96,1536]{1,0:T(8,128)(2,1)S(1)}, u32[]{:S(2)}, u32[]{:S(2)}) collective-permute-start(bf16[96,1536]{1,0:T(8,128)(2,1)S(1)} %get-tuple-element.70), channel_id=1, source_target_pairs={{0,96},{1,97},{2,98},{3,99},{4,28},{5,29},{6,30},{7,31},{8,104},{9... | collective-permute-start | bytes 884744 | tf_op jit(solution)/shard_map/ppermute | solution.py:69
  165.3 15.1 %collective-permute-start.20 = (bf16[128,1536]{1,0:T(8,128)(2,1)S(1)}, bf16[128,1536]{1,0:T(8,128)(2,1)S(1)}, u32[]{:S(2)}, u32[]{:S(2)}) collective-permute-start(bf16[128,1536]{1,0:T(8,128)(2,1)S(1)} %get-tuple-element.86), channel_id=1, source_target_pairs={{0,4},{1,5},{2,6},{3,7},{4,0},{5,1},{6,2},{7,3},{8,12},{9,13},{10,... | collective-permute-start | bytes 1179656 | tf_op jit(solution)/shard_map/ppermute | solution.py:69
  179.7 1.9 collective-permute-start.33
  180.4 2.2 %copy-start.11 = (f32[6,12,3072]{2,1,0:T(8,128)S(1)}, f32[6,12,3072]{2,1,0:T(8,128)}, u32[]{:S(2)}) copy-start(f32[6,12,3072]{2,1,0:T(8,128)} %one.1) | copy-start | bytes 2654212
  (13 other events, 18.6 us)
Sparse Core Ops, SparseCore 0:
  129.0 37.7 reduce-scatter.1
